TPU v7x, 128 devices: a whole 4x4x4 slice. The times are simulated.
128 devices in a mesh: eg: 32 (over x, y, core), tp: 4 (over z).
Axes of the slice: x: 4, y: 4, z: 4, core: 2. Of those that a mesh axis runs over, the one named last changes fastest.
Arguments:
- tokens: bfloat16 [8192, 2880], P(('eg', 'tp')), may hold values from -6 to 6
- routes: int32 [8192, 4], P(('eg', 'tp')), may hold values from 0 to 127, as said below
- combine: float32 [8192, 4], P(('eg', 'tp')), may hold values from 0.1 to 0.6
- gate_values: bfloat16 [128, 1440, 2880], P('tp', 'eg'), may hold values from -0.109375 to 0.109375
- gate_scales: bfloat16 [128, 1440, 90], P('tp', 'eg'), may hold values from 0.25 to 4
- up_values: bfloat16 [128, 1440, 2880], P('tp', 'eg'), may hold values from -0.109375 to 0.109375
- up_scales: bfloat16 [128, 1440, 90], P('tp', 'eg'), may hold values from 0.25 to 4
- down_values: bfloat16 [128, 1440, 2880], P('tp', 'eg'), may hold values from -0.15625 to 0.15625
- down_scales: bfloat16 [128, 1440, 90], P('tp', 'eg'), may hold values from 0.25 to 4
Outputs:
- combined: bfloat16 [8192, 2880], P(('eg', 'tp'))
Inputs may be any that keep to these rules, and one draw needn't show every extreme that they name: `routes`: each row names 4 different experts. In each aligned block of 64 rows exactly half of the experts are named, each by exactly 4 rows; one expert is named by 4 rows of every block.
All inputs are finite; a program needn't handle non-finite values.
Results may differ from a plain program's by a relative error of at most 0.0076.
Values may be sent and summed in bfloat16 or wider, within the bound.
A program may use at most 320 MiB of HBM per device.

v0:
```python
import jax
import jax.numpy as jnp
from jax import lax
from jax.sharding import PartitionSpec as P


def dequantize(values, scales):
    blocks = scales.shape[-1]
    shaped = values.reshape(values.shape[:-1] + (blocks, values.shape[-1] // blocks))
    scaled = shaped.astype(jnp.float32) * scales.astype(jnp.float32)[..., None]
    return scaled.reshape(values.shape).astype(jnp.bfloat16)


def expert_ffn(picked, w_gate, w_up, w_down):
    gate_part = lax.dot_general(
        picked, w_gate, (((1,), (1,)), ((), ())), preferred_element_type=jnp.float32
    )
    upward = lax.dot_general(
        picked, w_up, (((1,), (1,)), ((), ())), preferred_element_type=jnp.float32
    )
    hidden = (jax.nn.silu(gate_part) * upward).astype(jnp.bfloat16)
    result = jnp.dot(hidden, w_down, preferred_element_type=jnp.float32)
    return result.astype(jnp.bfloat16)


def local(
    tokens,
    routes,
    combine,
    gate_values,
    gate_scales,
    up_values,
    up_scales,
    down_values,
    down_scales,
):
    eg_count = lax.axis_size("eg")
    tp_count = lax.axis_size("tp")
    experts = eg_count * tp_count
    tok_rows, feature_dim = tokens.shape
    top_count = routes.shape[1]
    capacity = 2 * tok_rows * top_count // experts
    relayed = (
        lax.all_to_all(gate_values, "eg", split_axis=0, concat_axis=1, tiled=True),
        lax.all_to_all(gate_scales, "eg", split_axis=0, concat_axis=1, tiled=True),
        lax.all_to_all(up_values, "eg", split_axis=0, concat_axis=1, tiled=True),
        lax.all_to_all(up_scales, "eg", split_axis=0, concat_axis=1, tiled=True),
        lax.all_to_all(down_values, "eg", split_axis=0, concat_axis=1, tiled=True),
        lax.all_to_all(down_scales, "eg", split_axis=0, concat_axis=1, tiled=True),
    )
    w_gate = dequantize(relayed[0][0], relayed[1][0])
    w_up = dequantize(relayed[2][0], relayed[3][0])
    w_down = dequantize(relayed[4][0], relayed[5][0])
    owner_ids = routes % eg_count * tp_count + routes // eg_count
    flat_owner = owner_ids.reshape(-1)
    owner_lanes = jnp.arange(experts, dtype=jnp.int32)
    hit_marks = (flat_owner[:, None] == owner_lanes[None, :]).astype(jnp.int32)
    earlier = jnp.cumsum(hit_marks, axis=0) - hit_marks
    pair_ranks = jnp.sum(earlier * hit_marks, axis=1)
    slot_ids = (flat_owner * capacity + pair_ranks).reshape(tok_rows, top_count)
    positions = jnp.arange(experts * capacity, dtype=jnp.int32)
    chosen = slot_ids[:, :, None] == positions[None, None, :]
    placing = jnp.sum(chosen.astype(jnp.float32), axis=1).astype(jnp.bfloat16)
    weighing = jnp.sum(jnp.where(chosen, combine[:, :, None], 0.0), axis=1)
    packed = lax.dot_general(
        placing, tokens, (((0,), (0,)), ((), ())), preferred_element_type=jnp.float32
    ).astype(jnp.bfloat16)
    arrived = lax.all_to_all(
        packed.reshape(experts, capacity, feature_dim),
        ("eg", "tp"),
        split_axis=0,
        concat_axis=0,
        tiled=True,
    )
    picked = arrived.reshape(experts * capacity, feature_dim)
    result = expert_ffn(picked, w_gate, w_up, w_down)
    returned = lax.all_to_all(
        result.reshape(experts, capacity, feature_dim),
        ("eg", "tp"),
        split_axis=0,
        concat_axis=0,
        tiled=True,
    )
    returned = returned.reshape(experts * capacity, feature_dim)
    combined = jnp.dot(weighing, returned.astype(jnp.float32), precision=lax.Precision.HIGHEST)
    return combined.astype(jnp.bfloat16)


def solution(mesh):
    placed = (
        P(("eg", "tp"), None),
        P(("eg", "tp"), None),
        P(("eg", "tp"), None),
        P("tp", "eg", None),
        P("tp", "eg", None),
        P("tp", "eg", None),
        P("tp", "eg", None),
        P("tp", "eg", None),
        P("tp", "eg", None),
    )
    return jax.shard_map(
        local, mesh=mesh, in_specs=placed, out_specs=P(("eg", "tp"), None), check_vma=False
    )
```

profile of v0, /device:TPU:0, one launch (start us, length us, event | category | flops | bytes accessed | tf_op | source)
XLA Modules:
  0.0 757.3 jit_solution(8713334073072503216)
XLA Ops:
  1.9 7.4 all-to-all-start.2
  13.0 6.3 all-to-all-done.2
  19.3 3.9 all-to-all-start.4
  26.7 6.4 all-to-all-done.4
  33.2 4.6 all-to-all-start.6
  41.8 5.8 reshape.126
  47.7 10.9 %all-to-all-start = ((bf16[128,4,2880]{2,1,0:T(4,128)(2,1)}), bf16[128,4,2880]{2,1,0:T(4,128)(2,1)S(1)}, u32[]{:S(2)}, u32[]{:S(2)}) async-start(bf16[128,4,2880]{2,1,0:T(4,128)(2,1)} %reshape.126), calls=%async_computation | async-start | bytes 6029312 | tf_op jit(solution)/shard_map/all_to_all | solution.py:68
  58.7 9.6 %copy.81 = bf16[32,45,2880]{2,1,0:T(8,128)(2,1)} copy(bf16[32,45,2880]{2,0,1:T(8,128)(2,1)} %param.12) | data formatting | bytes 16588800 | tf_op args[3]
  68.2 30.4 %all-to-all-done = bf16[128,4,2880]{2,1,0:T(4,128)(2,1)S(1)} async-done(((bf16[128,4,2880]{2,1,0:T(4,128)(2,1)}), bf16[128,4,2880]{2,1,0:T(4,128)(2,1)S(1)}, u32[]{:S(2)}, u32[]{:S(2)}) %all-to-all-start) | async-done | bytes 2949152 | tf_op jit(solution)/shard_map/all_to_all | solution.py:68
  98.6 5.0 all-to-all-start.1
  103.6 9.7 %copy.86 = bf16[32,45,2880]{2,1,0:T(8,128)(2,1)} copy(bf16[32,45,2880]{2,0,1:T(8,128)(2,1)} %param.14) | data formatting | bytes 16588800 | tf_op args[5]
  113.3 113.5 %all-to-all-done.1 = bf16[32,45,2880]{2,1,0:T(8,128)(2,1)} async-done(((bf16[32,45,2880]{2,1,0:T(8,128)(2,1)}), bf16[32,45,2880]{2,1,0:T(8,128)(2,1)}, u32[]{:S(2)}, u32[]{:S(2)}) %all-to-all-start.1) | async-done | bytes 8294432 | tf_op jit(solution)/shard_map/all_to_all | solution.py:44
  226.8 31.8 %all-to-all-start.3 = ((bf16[32,45,2880]{2,1,0:T(8,128)(2,1)}), bf16[32,45,2880]{2,1,0:T(8,128)(2,1)}, u32[]{:S(2)}, u32[]{:S(2)}) async-start(bf16[32,45,2880]{2,1,0:T(8,128)(2,1)} %copy.86), calls=%async_computation.3 | async-start | bytes 18087936 | tf_op jit(solution)/shard_map/all_to_all | solution.py:46
  258.6 9.5 %copy.91 = bf16[32,45,2880]{2,1,0:T(8,128)(2,1)} copy(bf16[32,45,2880]{2,0,1:T(8,128)(2,1)} %param.16) | data formatting | bytes 16588800 | tf_op args[7]
  268.1 113.6 %all-to-all-done.3 = bf16[32,45,2880]{2,1,0:T(8,128)(2,1)} async-done(((bf16[32,45,2880]{2,1,0:T(8,128)(2,1)}), bf16[32,45,2880]{2,1,0:T(8,128)(2,1)}, u32[]{:S(2)}, u32[]{:S(2)}) %all-to-all-start.3) | async-done | bytes 8294432 | tf_op jit(solution)/shard_map/all_to_all | solution.py:46
  381.7 21.8 %all-to-all-start.5 = ((bf16[32,45,2880]{2,1,0:T(8,128)(2,1)}), bf16[32,45,2880]{2,1,0:T(8,128)(2,1)}, u32[]{:S(2)}, u32[]{:S(2)}) async-start(bf16[32,45,2880]{2,1,0:T(8,128)(2,1)} %copy.91), calls=%async_computation.5 | async-start | bytes 18087936 | tf_op jit(solution)/shard_map/all_to_all | solution.py:48
  416.1 9.4 %mul.75 = f32[1440,90,32]{0,2,1:T(8,128)} broadcast(f32[1440,90]{0,1:T(8,128)} %copy.93), dimensions={0,1} | broadcast | bytes 17107200 | tf_op jit(solution)/shard_map/mul | solution.py:10
  425.5 17.8 %copy.94 = f32[1440,2880]{1,0:T(8,128)} copy(f32[1440,2880]{0,1:T(8,128)} %bitcast.28) | data formatting | bytes 33177600 | tf_op jit(solution)/shard_map/mul | solution.py:10
  446.2 11.6 %copy_convert_fusion.1 = f32[32,45,2880]{2,0,1:T(8,128)} fusion(bf16[32,45,2880]{2,1,0:T(8,128)(2,1)} %all-to-all-done.1), kind=kLoop, calls=%fused_computation.5 | loop fusion | flops 4147200 | bytes 24883200 | tf_op jit(solution)/shard_map/convert_element_type | solution.py:10
  457.8 39.1 %copy.83 = f32[32,45,2880]{1,0,2:T(8,128)} copy(f32[32,45,2880]{2,0,1:T(8,128)} %copy_convert_fusion.1) | data formatting | bytes 33177600 | tf_op jit(solution)/shard_map/convert_element_type | solution.py:10
  497.0 42.9 %reshape.130 = f32[1440,90,32]{0,2,1:T(8,128)} reshape(f32[32,45,2880]{1,0,2:T(8,128)} %copy.83) | data formatting | bytes 33177600 | tf_op jit(solution)/shard_map/convert_element_type | solution.py:10
  539.8 11.7 %copy_convert_fusion = f32[32,45,2880]{2,0,1:T(8,128)} fusion(bf16[32,45,2880]{2,1,0:T(8,128)(2,1)} %all-to-all-done.3), kind=kLoop, calls=%fused_computation.4 | loop fusion | flops 4147200 | bytes 24883200 | tf_op jit(solution)/shard_map/convert_element_type | solution.py:10
  551.5 39.1 %copy.88 = f32[32,45,2880]{1,0,2:T(8,128)} copy(f32[32,45,2880]{2,0,1:T(8,128)} %copy_convert_fusion) | data formatting | bytes 33177600 | tf_op jit(solution)/shard_map/convert_element_type | solution.py:10
  590.7 42.9 %reshape.132 = f32[1440,90,32]{0,2,1:T(8,128)} reshape(f32[32,45,2880]{1,0,2:T(8,128)} %copy.88) | data formatting | bytes 33177600 | tf_op jit(solution)/shard_map/convert_element_type | solution.py:10
  633.6 7.9 %multiply_convert_fusion.1 = bf16[1440,90,32]{0,2,1:T(8,128)(2,1)S(1)} fusion(f32[1440,90,32]{0,2,1:T(8,128)} %reshape.130, f32[1440,90]{0,1:T(8,128)} %copy.85), kind=kLoop, calls=%fused_computation.1 | loop fusion | flops 8294400 | bytes 25401600 | tf_op jit(solution)/shard_map/convert_element_type | solution.py:11
  641.5 6.5 fusion.16
  648.0 10.3 %multiply_convert_fusion = bf16[1440,90,32]{0,2,1:T(8,128)(2,1)} fusion(f32[1440,90,32]{0,2,1:T(8,128)} %reshape.132, f32[1440,90]{0,1:T(8,128)S(1)} %copy-done.3), kind=kLoop, calls=%fused_computation | loop fusion | flops 8294400 | bytes 25401600 | tf_op jit(solution)/shard_map/convert_element_type | solution.py:11
  658.4 17.8 %reshape.134 = f32[1440,2880]{1,0:T(8,128)} reshape(bf16[32,45,2880]{2,1,0:T(8,128)(2,1)} %all-to-all-done.5) | data formatting | bytes 24883200 | tf_op jit(solution)/shard_map/convert_element_type | solution.py:10
  676.2 19.9 %fusion.1 = bf16[512,2880]{0,1:T(8,128)(2,1)} fusion(f32[1440,2880]{1,0:T(8,128)} %reshape.134, f32[1440,2880]{1,0:T(8,128)} %copy.94, bf16[512,2880]{1,0:T(8,128)(2,1)S(1)} %copy-done.2, bf16[1440,2880]{0,1:T(8,128)(2,1)} %bitcast.29, f32[512,1440]{0,1:T(8,128)} %fusion.16), kind=kOutput, calls=%fused_computation.6 | convolution fusion | flops 8507658240 | bytes 50319360 | tf_op jit(solution)/shard_map/dot_general | solution.py:22
  696.1 3.3 copy.95
  701.9 48.3 %all_to_all.64 = bf16[128,4,2880]{2,1,0:T(4,128)(2,1)} all-to-all(bf16[128,4,2880]{2,1,0:T(4,128)(2,1)} %reshape.128), channel_id=1, replica_groups=mesh['eg'=32,'tp'=4] {'eg','tp'}, dimensions={0} | all-to-all | bytes 5898240 | tf_op jit(solution)/shard_map/all_to_all | solution.py:77
  750.1 4.4 reshape.129
  (47 shorter events, 33.4 us)
Async XLA Ops:
  0.0 37.8 %copy-start = (bf16[64,2880]{1,0:T(8,128)(2,1)S(1)}, bf16[64,2880]{1,0:T(8,128)(2,1)}, u32[]{:S(2)}) copy-start(bf16[64,2880]{1,0:T(8,128)(2,1)} %param.9) | copy-start | bytes 1105924
  1.9 17.4 %all-to-all-start.2 = ((bf16[32,45,90]{2,1,0:T(8,128)(2,1)}), bf16[32,45,90]{2,1,0:T(8,128)(2,1)S(1)}, u32[]{:S(2)}, u32[]{:S(2)}) async-start(bf16[32,45,90]{2,1,0:T(8,128)(2,1)} %copy.84), calls=%async_computation.2 | async-start | bytes 786432 | tf_op jit(solution)/shard_map/all_to_all | solution.py:45
  19.3 18.5 %copy-start.4 = (bf16[32,45,90]{2,1,0:T(8,128)(2,1)}, bf16[32,45,90]{2,1,0:T(8,128)(2,1)S(1)}, u32[]{:S(2)}) copy-start(bf16[32,45,90]{2,1,0:T(8,128)(2,1)S(1)} %all-to-all-done.2) | copy-start | bytes 777604
  19.3 13.9 %all-to-all-start.4 = ((bf16[32,45,90]{2,1,0:T(8,128)(2,1)}), bf16[32,45,90]{2,1,0:T(8,128)(2,1)S(1)}, u32[]{:S(2)}, u32[]{:S(2)}) async-start(bf16[32,45,90]{2,1,0:T(8,128)(2,1)} %copy.89), calls=%async_computation.4 | async-start | bytes 786432 | tf_op jit(solution)/shard_map/all_to_all | solution.py:47
  33.2 4.6 copy-start.5
  33.2 14.5 %all-to-all-start.6 = ((bf16[32,45,90]{2,1,0:T(8,128)(2,1)}), bf16[32,45,90]{2,1,0:T(8,128)(2,1)}, u32[]{:S(2)}, u32[]{:S(2)}) async-start(bf16[32,45,90]{2,1,0:T(8,128)(2,1)} %copy.92), calls=%async_computation.6 | async-start | bytes 786432 | tf_op jit(solution)/shard_map/all_to_all | solution.py:49
  47.7 50.9 %all-to-all-start = ((bf16[128,4,2880]{2,1,0:T(4,128)(2,1)}), bf16[128,4,2880]{2,1,0:T(4,128)(2,1)S(1)}, u32[]{:S(2)}, u32[]{:S(2)}) async-start(bf16[128,4,2880]{2,1,0:T(4,128)(2,1)} %reshape.126), calls=%async_computation | async-start | bytes 6029312 | tf_op jit(solution)/shard_map/all_to_all | solution.py:68
  98.6 128.1 %all-to-all-start.1 = ((bf16[32,45,2880]{2,1,0:T(8,128)(2,1)}), bf16[32,45,2880]{2,1,0:T(8,128)(2,1)}, u32[]{:S(2)}, u32[]{:S(2)}) async-start(bf16[32,45,2880]{2,1,0:T(8,128)(2,1)} %copy.81), calls=%async_computation.1 | async-start | bytes 18087936 | tf_op jit(solution)/shard_map/all_to_all | solution.py:44
  226.8 154.9 %all-to-all-start.3 = ((bf16[32,45,2880]{2,1,0:T(8,128)(2,1)}), bf16[32,45,2880]{2,1,0:T(8,128)(2,1)}, u32[]{:S(2)}, u32[]{:S(2)}) async-start(bf16[32,45,2880]{2,1,0:T(8,128)(2,1)} %copy.86), calls=%async_computation.3 | async-start | bytes 18087936 | tf_op jit(solution)/shard_map/all_to_all | solution.py:46
  381.7 276.7 %all-to-all-start.5 = ((bf16[32,45,2880]{2,1,0:T(8,128)(2,1)}), bf16[32,45,2880]{2,1,0:T(8,128)(2,1)}, u32[]{:S(2)}, u32[]{:S(2)}) async-start(bf16[32,45,2880]{2,1,0:T(8,128)(2,1)} %copy.91), calls=%async_computation.5 | async-start | bytes 18087936 | tf_op jit(solution)/shard_map/all_to_all | solution.py:48
  633.6 7.9 %copy-start.2 = (bf16[512,2880]{1,0:T(8,128)(2,1)S(1)}, bf16[512,2880]{1,0:T(8,128)(2,1)}, u32[]{:S(2)}) copy-start(bf16[512,2880]{1,0:T(8,128)(2,1)} %reshape.127) | copy-start | bytes 8847364
  641.5 6.5 copy-start.3
  699.4 55.1 %copy-start.6 = (f32[64,512]{1,0:T(8,128)S(1)}, f32[64,512]{1,0:T(8,128)}, u32[]{:S(2)}) copy-start(f32[64,512]{1,0:T(8,128)} %get-tuple-element.6) | copy-start | bytes 393220
  699.4 57.5 %copy-start.1 = (bf16[64,2880]{1,0:T(8,128)(2,1)S(1)}, bf16[64,2880]{1,0:T(8,128)(2,1)}, u32[]{:S(2)}) copy-start(bf16[64,2880]{1,0:T(8,128)(2,1)} %param.9) | copy-start | bytes 1105924
where the time goes:
time: 772 us; the launch traced here: 757 us
  local copies, waits for them, and re-layouts  279 us (36%)
  waiting for transfers between devices  270 us (35%)
  starting transfers between devices  85.5 us (11%)
  blocking collectives  48.3 us (6%)
  other arithmetic  43.6 us (6%)
  matrix products  29.8 us (4%)
    convert_element_type x11, local copies, waits for them, and re-layouts, dequantize(): scaled = shaped.astype(jnp.float32) * scales.astype(jnp.float32)[..., None]  194 us
    all_to_all x1, waiting for transfers between devices, local(): lax.all_to_all(up_values, 'eg', split_axis=0, concat_axis=1, tiled=True)  114 us
    all_to_all x1, waiting for transfers between devices, local(): lax.all_to_all(gate_values, 'eg', split_axis=0, concat_axis=1, tiled=True)  113 us
    all_to_all x1, blocking collectives, local(): lax.all_to_all(result.reshape(experts, capacity, feature_dim), ('eg', 'tp...  48.3 us
    unnamed x22, local copies, waits for them, and re-layouts  35.3 us
    all_to_all x1, starting transfers between devices, local(): lax.all_to_all(up_values, 'eg', split_axis=0, concat_axis=1, tiled=True)  31.8 us
    all_to_all x1, waiting for transfers between devices, local(): lax.all_to_all(packed.reshape(experts, capacity, feature_dim), ('eg', 'tp...  30.4 us
    mul x2, local copies, waits for them, and re-layouts, dequantize(): scaled = shaped.astype(jnp.float32) * scales.astype(jnp.float32)[..., None]  27.2 us
  transfers between devices with their start and end apart: 7, of which 6 were waited for; matrix products, arithmetic and copies ran while one was open for 40% of the time, Pallas kernels for 0%

commit v1 on v0

v1 whole, which is shorter than its diff:
```python
import functools

import jax
import jax.numpy as jnp
from jax import lax
from jax.experimental import pallas as pl
from jax.experimental.pallas import tpu as pltpu
from jax.sharding import PartitionSpec as P

MESH = pl.DeviceIdType.MESH
ANY = pl.BlockSpec(memory_space=pl.ANY)
BF16, F32 = jnp.bfloat16, jnp.float32

D, FS, EXP, ROWS = 2880, 45, 32, 64
PARTS, PW = 3, 1024
FP = 48
META = 896
BLOCK = 32
VMEM = 62 * 1024 * 1024


def position():
    eg, z = lax.axis_index("eg"), lax.axis_index("tp")
    return (eg // 8, (eg // 2) % 4, z), eg % 2


def device(at, core):
    return ((at[0] * 4 + at[1]) * 2 + core, at[2])


def moved(at, axis, by):
    at = list(at)
    at[axis] = (at[axis] + by + 4) % 4
    return tuple(at)


def greet(at, core, sibling):
    barrier = pltpu.get_barrier_semaphore()
    for axis in range(3):
        for way in (1, -1):
            pl.semaphore_signal(
                barrier, inc=1, device_id=device(moved(at, axis, way), core), device_id_type=MESH
            )
    if sibling:
        pl.semaphore_signal(barrier, inc=1, device_id=device(at, 1 - core), device_id_type=MESH)
    pl.semaphore_wait(barrier, 7 if sibling else 6)


def dequantize_kernel(gv, gs, uv, us, dv, ds, out, flat):
    step = pl.program_id(0)
    width = gv.shape[-1]
    blocks = gs.shape[-1]
    lane = lax.broadcasted_iota(jnp.int32, (blocks, width), 1) + step * width
    spread = (lane // BLOCK == lax.broadcasted_iota(jnp.int32, (blocks, width), 0)).astype(BF16)
    inside = lax.broadcasted_iota(jnp.int32, (EXP, width), 1) + step * width < D
    for which, (values, scales) in enumerate(((gv, gs), (uv, us), (dv, ds))):
        def unit(f, _):
            scale = jnp.dot(scales[f], spread, preferred_element_type=F32)
            full = jnp.where(inside, values[f].astype(F32) * scale, 0.0)
            for c in range(width // 128):
                flat[c, pl.ds(f * EXP, EXP), :] = full[:, c * 128 : (c + 1) * 128]
            return 0

        lax.fori_loop(0, FS, unit, 0, unroll=5)

        def expert(e, _):
            rows = jnp.concatenate(
                [flat[c, pl.ds(e, FS, stride=EXP), :] for c in range(width // 128)], axis=1
            )
            rows = jnp.concatenate([rows, jnp.zeros((FP - FS, width), F32)], axis=0)
            out[e, which] = rows.astype(BF16)
            return 0

        lax.fori_loop(0, EXP, expert, 0, unroll=4)


def dequantize(gv, gs, uv, us, dv, ds):
    width = 512
    value = pl.BlockSpec((FS, EXP, width), lambda i: (0, 0, i))
    scale = pl.BlockSpec((FS, EXP, D // BLOCK), lambda i: (0, 0, 0))
    return pl.pallas_call(
        dequantize_kernel,
        grid=(PARTS * PW // width,),
        out_shape=jax.ShapeDtypeStruct((EXP, 3, FP, PARTS * PW), BF16),
        in_specs=[value, scale] * 3,
        out_specs=pl.BlockSpec((EXP, 3, FP, width), lambda i: (0, 0, 0, i)),
        scratch_shapes=[pltpu.VMEM((width // 128, FS * EXP, 128), F32)],
        compiler_params=pltpu.CompilerParams(vmem_limit_bytes=VMEM),
    )(gv, gs, uv, us, dv, ds)


def gather_kernel(tok, own_w, every, w1, w2, ssem, rsem, lsem, wsem):
    me, core = position()
    greet(me, core, True)
    pieces = []
    for i, (source, target, first) in enumerate(((0, w1, 0), (1, w1, 128), (2, w2, 0))):
        pieces.append(
            pltpu.make_async_remote_copy(
                own_w.at[:, source],
                target.at[:, pl.ds(first + FP, FP)],
                wsem.at[0, i],
                wsem.at[1, i],
                device_id=device(me, 1 - core),
                device_id_type=MESH,
            )
        )
        pieces.append(
            pltpu.make_async_copy(own_w.at[:, source], target.at[:, pl.ds(first, FP)], wsem.at[2, i])
        )
    for piece in pieces:
        piece.start()
    own = [
        pltpu.make_async_copy(tok.at[p], every.at[p, me[0], me[1], me[2]], lsem.at[p])
        for p in range(PARTS)
    ]
    for c in own:
        c.start()

    def region(p, phase, j, source, half):
        order = [p, (p + 1) % 3, (p + 2) % 3]
        index = [slice(None)] * 3
        index[order[phase]] = source
        if phase == 0:
            index[order[1]], index[order[2]] = me[order[1]], me[order[2]]
        elif phase == 1:
            index[order[2]] = me[order[2]]
        else:
            index[order[1]] = j
        rows = slice(None) if half is None else pl.ds(half * 32, 32)
        return every.at[(p, *index, rows)]

    def describe(p, phase, jj, way, step, arriving):
        axis = (p + phase) % 3
        back = way * (step + (1 if arriving else 0))
        source = (me[axis] - back + 8) % 4
        half = None if step == 0 else (0 if way == 1 else 1)
        j = None if phase < 2 else (me[(p + 1) % 3] + (0, -1, 1, 2)[jj] + 4) % 4
        there = region(p, phase, j, source, half)
        here = tok.at[p] if phase == 0 and step == 0 else there
        slot, kind = phase + jj, (0 if way == 1 else 1) + 2 * step
        return pltpu.make_async_remote_copy(
            here,
            there,
            ssem.at[p, slot, kind],
            rsem.at[p, slot, kind],
            device_id=device(moved(me, axis, way), core),
            device_id_type=MESH,
        )

    sent = []

    def go(p, phase, jj, way, step):
        c = describe(p, phase, jj, way, step, False)
        c.start()
        sent.append(c)

    def arrive(p, phase, jj, way, step):
        describe(p, phase, jj, way, step, True).wait_recv()

    parts, ways = range(PARTS), (1, -1)
    for p in parts:
        for way in ways:
            go(p, 0, 0, way, 0)
    for p in parts:
        for way in ways:
            arrive(p, 0, 0, way, 0)
            go(p, 0, 0, way, 1)
    for c in own:
        c.wait()
    for p in parts:
        for way in ways:
            arrive(p, 0, 0, way, 1)
        for way in ways:
            go(p, 1, 0, way, 0)
    for p in parts:
        for way in ways:
            go(p, 2, 0, way, 0)
    for p in parts:
        for way in ways:
            arrive(p, 1, 0, way, 0)
            go(p, 1, 0, way, 1)
    for p in parts:
        for jj in (1, 2):
            for way in ways:
                go(p, 2, jj, way, 0)
    for p in parts:
        for way in ways:
            arrive(p, 1, 0, way, 1)
        for way in ways:
            go(p, 2, 3, way, 0)
    for jj in range(4):
        for p in parts:
            for way in ways:
                arrive(p, 2, jj, way, 0)
                go(p, 2, jj, way, 1)
    for jj in range(4):
        for p in parts:
            for way in ways:
                arrive(p, 2, jj, way, 1)
    for c in sent:
        c.wait_send()
    for piece in pieces:
        piece.wait()


def gather(tok, own_w):
    return pl.pallas_call(
        gather_kernel,
        out_shape=[
            jax.ShapeDtypeStruct((PARTS, 4, 4, 4, ROWS, PW), BF16),
            jax.ShapeDtypeStruct((EXP, 256, PARTS * PW), BF16),
            jax.ShapeDtypeStruct((EXP, 2 * FP, PARTS * PW), BF16),
        ],
        in_specs=[ANY] * 2,
        out_specs=[ANY] * 3,
        scratch_shapes=[
            pltpu.SemaphoreType.DMA((PARTS, 6, 4)),
            pltpu.SemaphoreType.DMA((PARTS, 6, 4)),
            pltpu.SemaphoreType.DMA((PARTS,)),
            pltpu.SemaphoreType.DMA((3, 3)),
        ],
        compiler_params=pltpu.CompilerParams(collective_id=1, has_side_effects=True),
    )(tok, own_w)


PER_STEP = 4


def upward_kernel(every, meta, w1, hidden, place, rows, acc):
    p, step = pl.program_id(0), pl.program_id(1)
    z = lax.axis_index("tp")

    @pl.when((p == 0) & (step == 0))
    def _():
        slots = lax.broadcasted_iota(jnp.int32, (ROWS, EXP * 16), 1).astype(F32)

        def block(i, _):
            g, b = i // 4, i % 4
            m = meta[0, g // 4, g % 4, b].astype(F32)
            local = m[:, 0:4] - (z * EXP).astype(F32)
            ids = local * 16.0 + b.astype(F32) * 4.0 + m[:, 4:8]
            ids = jnp.where((local >= 0.0) & (local < EXP), ids, -1.0)
            hit = slots == ids[:, 0:1]
            for k in range(1, 4):
                hit = hit | (slots == ids[:, k : k + 1])
            place[g, pl.ds(b * ROWS, ROWS), :] = hit.astype(F32).astype(BF16)
            return 0

        lax.fori_loop(0, 64, block, 0)

    @pl.when(step == 0)
    def _():
        def group(g, _):
            x = every[0, g // 4, g % 4].reshape(4 * ROWS, PW)
            picked = lax.dot_general(
                place[g], x, (((0,), (0,)), ((), ())), preferred_element_type=F32
            )
            rows[:, pl.ds(g * 16, 16), :] = picked.astype(BF16).reshape(EXP, 16, PW)
            return 0

        lax.fori_loop(0, 16, group, 0)

    for i in range(PER_STEP):
        e = step * PER_STEP + i
        out = lax.dot_general(
            rows[e], w1[i], (((1,), (1,)), ((), ())), preferred_element_type=F32
        )

        @pl.when(p == 0)
        def _():
            acc[e] = out

        @pl.when(p == 1)
        def _():
            acc[e] += out

        @pl.when(p == 2)
        def _():
            total = acc[e] + out
            gate, up = total[:, :128], total[:, 128:]
            made = gate / (1.0 + jnp.exp(-gate)) * up
            m = rows[e, :, META:].astype(F32)
            named = (m[:, 0:4] == (z * EXP + e).astype(F32)).astype(F32)
            weights = [
                jnp.sum(m[:, 8 + 4 * i : 12 + 4 * i] * named, axis=1, keepdims=True)
                for i in range(3)
            ]
            lane = lax.broadcasted_iota(jnp.int32, made.shape, 1)
            for i in range(3):
                made = jnp.where(lane == 96 + i, weights[i], made)
            made = jnp.where(lane > 98, 0.0, made)
            hidden[e] = made.astype(BF16)


def upward(every, w1):
    return pl.pallas_call(
        upward_kernel,
        grid=(PARTS, EXP // PER_STEP),
        out_shape=[
            jax.ShapeDtypeStruct((EXP, 256, 128), BF16),
            jax.ShapeDtypeStruct((16, 4 * ROWS, EXP * 16), BF16),
        ],
        in_specs=[
            pl.BlockSpec((1, 4, 4, 4, ROWS, PW), lambda p, s: (p, 0, 0, 0, 0, 0)),
            pl.BlockSpec((1, 4, 4, 4, ROWS, 128), lambda p, s: (2, 0, 0, 0, 0, 7)),
            pl.BlockSpec((PER_STEP, 256, PW), lambda p, s: (s, 0, p)),
        ],
        out_specs=[
            pl.BlockSpec((EXP, 256, 128), lambda p, s: (0, 0, 0)),
            pl.BlockSpec((16, 4 * ROWS, EXP * 16), lambda p, s: (0, 0, 0)),
        ],
        scratch_shapes=[
            pltpu.VMEM((EXP, 256, PW), BF16),
            pltpu.VMEM((EXP, 256, 256), F32),
        ],
        compiler_params=pltpu.CompilerParams(vmem_limit_bytes=VMEM),
    )(every, every, w1)


def downward_kernel(hidden, place, w2, out, results):
    step = pl.program_id(1)
    for i in range(PER_STEP):
        e = step * PER_STEP + i
        h = hidden[e]
        w = h[:, 96:99].astype(F32)
        w = (w[:, 0:1] + w[:, 1:2]) + w[:, 2:3]
        y = jnp.dot(h[:, : 2 * FP], w2[i], preferred_element_type=F32) * w
        results[:, pl.ds(e * 16, 16), :] = y.astype(BF16).reshape(16, 16, PW)

    @pl.when(step == EXP // PER_STEP - 1)
    def _():
        def group(g, _):
            summed = jnp.dot(place[g], results[g], preferred_element_type=F32)
            out[0, g // 4, g % 4] = summed.astype(BF16).reshape(4, ROWS, PW)
            return 0

        lax.fori_loop(0, 16, group, 0)


def downward(hidden, place, w2):
    return pl.pallas_call(
        downward_kernel,
        grid=(PARTS, EXP // PER_STEP),
        out_shape=jax.ShapeDtypeStruct((PARTS, 4, 4, 4, ROWS, PW), BF16),
        in_specs=[
            pl.BlockSpec((EXP, 256, 128), lambda p, s: (0, 0, 0)),
            pl.BlockSpec((16, 4 * ROWS, EXP * 16), lambda p, s: (0, 0, 0)),
            pl.BlockSpec((PER_STEP, 2 * FP, PW), lambda p, s: (s, 0, p)),
        ],
        out_specs=pl.BlockSpec((1, 4, 4, 4, ROWS, PW), lambda p, s: (p, 0, 0, 0, 0, 0)),
        scratch_shapes=[pltpu.VMEM((16, EXP * 16, PW), BF16)],
        compiler_params=pltpu.CompilerParams(vmem_limit_bytes=VMEM),
    )(hidden, place, w2)


def scatter_kernel(part, out, far0, near0, mid0, acc, far1, near1, far2, near2, own2, sems, lsem):
    me, core = position()
    greet(me, core, False)
    parts = range(PARTS)
    sent = []

    def copy(here, there, p, phase, jj, kind, way, axis):
        return pltpu.make_async_remote_copy(
            here,
            there,
            sems.at[0, p, phase + jj, kind],
            sems.at[1, p, phase + jj, kind],
            device_id=device(moved(me, axis, way), core),
            device_id_type=MESH,
        )

    def go(*a):
        c = copy(*a)
        c.start()
        sent.append(c)

    def j_of(p, jj):
        return (me[(p + 1) % 3] + (2, 1, -1, 0)[jj] + 4) % 4

    def piece(p, jj, by, rows):
        o0, o1, o2 = p, (p + 1) % 3, (p + 2) % 3
        index = [slice(None)] * 3
        index[o1] = j_of(p, jj)
        index[o2] = (me[o2] + by + 4) % 4
        return part.at[(p, *index, rows)]

    top, bottom, whole = pl.ds(0, 32), pl.ds(32, 32), slice(None)

    def load(p, jj, k):
        by, rows = ((1, top), (-1, bottom), (0, whole))[k]
        there = acc.at[p, jj] if k == 2 else mid0.at[p, jj, k]
        return pltpu.make_async_copy(piece(p, jj, by, rows), there, lsem.at[p, jj, k])

    def issue(jj):
        for p in parts:
            axis = (p + 2) % 3
            go(piece(p, jj, 2, top), far0.at[p, jj, 0], p, 0, jj, 0, 1, axis)
            go(piece(p, jj, 2, bottom), far0.at[p, jj, 1], p, 0, jj, 1, -1, axis)
            for k in range(3):
                load(p, jj, k).start()
        for p in parts:
            axis = (p + 2) % 3
            go(piece(p, jj, 1, bottom), near0.at[p, jj, 0, :, bottom], p, 0, jj, 2, 1, axis)
            go(piece(p, jj, -1, top), near0.at[p, jj, 1, :, top], p, 0, jj, 3, -1, axis)

    def wait_in(there, p, phase, jj, kind, axis):
        copy(there, there, p, phase, jj, kind, 1, axis).wait_recv()

    def add(target, *others):
        count = target.shape[0]

        def one(i, _):
            total = target[i].astype(F32)
            for other in others:
                total = total + other[i].astype(F32)
            target[i] = total.astype(BF16)
            return 0

        lax.fori_loop(0, count, one, 0)

    def middle(jj):
        for p in parts:
            axis = (p + 2) % 3
            for k, way in ((0, 1), (1, -1)):
                half = top if k == 0 else bottom
                load(p, jj, k).wait()
                wait_in(far0.at[p, jj, k], p, 0, jj, k, axis)
                add(mid0.at[p, jj, k], far0.at[p, jj, k])
                go(mid0.at[p, jj, k], near0.at[p, jj, k, :, half], p, 0, jj, 4 + k, way, axis)

    def finish(jj):
        for p in parts:
            axis = (p + 2) % 3
            load(p, jj, 2).wait()
            wait_in(near0.at[p, jj, 0, :, bottom], p, 0, jj, 2, axis)
            wait_in(near0.at[p, jj, 1, :, top], p, 0, jj, 3, axis)
            wait_in(near0.at[p, jj, 0, :, top], p, 0, jj, 4, axis)
            wait_in(near0.at[p, jj, 1, :, bottom], p, 0, jj, 5, axis)
            add(acc.at[p, jj], near0.at[p, jj, 0], near0.at[p, jj, 1])
            axis = (p + 1) % 3
            if jj == 0:
                go(acc.at[p, 0, :, top], far1.at[p, 0], p, 4, 0, 0, 1, axis)
                go(acc.at[p, 0, :, bottom], far1.at[p, 1], p, 4, 0, 1, -1, axis)
            elif jj == 1:
                go(acc.at[p, 1, :, bottom], near1.at[p, 0, :, bottom], p, 4, 0, 2, 1, axis)
            elif jj == 2:
                go(acc.at[p, 2, :, top], near1.at[p, 1, :, top], p, 4, 0, 3, -1, axis)
        if jj in (1, 2):
            k, way, half = (0, 1, top) if jj == 1 else (1, -1, bottom)
            for p in parts:
                axis = (p + 1) % 3
                wait_in(far1.at[p, k], p, 4, 0, k, axis)
                add(acc.at[p, jj, :, half], far1.at[p, k])
                go(acc.at[p, jj, :, half], near1.at[p, k, :, half], p, 4, 0, 4 + k, way, axis)

    issue(0)
    issue(1)
    for jj in range(4):
        middle(jj)
        if jj + 2 < 4:
            issue(jj + 2)
        if jj >= 1:
            finish(jj - 1)
    finish(3)
    for p in parts:
        axis = (p + 1) % 3
        wait_in(near1.at[p, 0, :, bottom], p, 4, 0, 2, axis)
        wait_in(near1.at[p, 1, :, top], p, 4, 0, 3, axis)
        wait_in(near1.at[p, 0, :, top], p, 4, 0, 4, axis)
        wait_in(near1.at[p, 1, :, bottom], p, 4, 0, 5, axis)
        add(acc.at[p, 3], near1.at[p, 0], near1.at[p, 1])
        t = [(me[p] + by + 4) % 4 for by in (2, 1, -1, 0)]
        go(acc.at[p, 3, t[0], top], far2.at[p, 0], p, 5, 0, 0, 1, p)
        go(acc.at[p, 3, t[0], bottom], far2.at[p, 1], p, 5, 0, 1, -1, p)
        go(acc.at[p, 3, t[1], bottom], near2.at[p, 0, bottom], p, 5, 0, 2, 1, p)
        go(acc.at[p, 3, t[2], top], near2.at[p, 1, top], p, 5, 0, 3, -1, p)
    for p in parts:
        t = [(me[p] + by + 4) % 4 for by in (2, 1, -1, 0)]
        for k, way, half in ((0, 1, top), (1, -1, bottom)):
            wait_in(far2.at[p, k], p, 5, 0, k, p)
            own2[p, k] = (
                acc[p, 3, t[1 + k], half].astype(F32) + far2[p, k].astype(F32)
            ).astype(BF16)
            go(own2.at[p, k], near2.at[p, k, half], p, 5, 0, 4 + k, way, p)
    for p in parts:
        wait_in(near2.at[p, 0, bottom], p, 5, 0, 2, p)
        wait_in(near2.at[p, 1, top], p, 5, 0, 3, p)
        wait_in(near2.at[p, 0, top], p, 5, 0, 4, p)
        wait_in(near2.at[p, 1, bottom], p, 5, 0, 5, p)
        out[p] = (
            acc[p, 3, me[p]].astype(F32) + near2[p, 0].astype(F32) + near2[p, 1].astype(F32)
        ).astype(BF16)
    for c in sent:
        c.wait_send()


def scatter(part):
    half = ROWS // 2
    return pl.pallas_call(
        scatter_kernel,
        out_shape=jax.ShapeDtypeStruct((PARTS, ROWS, PW), BF16),
        in_specs=[ANY],
        out_specs=pl.BlockSpec(memory_space=pltpu.VMEM),
        scratch_shapes=[
            pltpu.VMEM((PARTS, 4, 2, 4, half, PW), BF16),
            pltpu.VMEM((PARTS, 4, 2, 4, ROWS, PW), BF16),
            pltpu.VMEM((PARTS, 4, 2, 4, half, PW), BF16),
            pltpu.VMEM((PARTS, 4, 4, ROWS, PW), BF16),
            pltpu.VMEM((PARTS, 2, 4, half, PW), BF16),
            pltpu.VMEM((PARTS, 2, 4, ROWS, PW), BF16),
            pltpu.VMEM((PARTS, 2, half, PW), BF16),
            pltpu.VMEM((PARTS, 2, ROWS, PW), BF16),
            pltpu.VMEM((PARTS, 2, half, PW), BF16),
            pltpu.SemaphoreType.DMA((2, PARTS, 6, 6)),
            pltpu.SemaphoreType.DMA((PARTS, 4, 3)),
        ],
        compiler_params=pltpu.CompilerParams(
            collective_id=2, has_side_effects=True, vmem_limit_bytes=VMEM
        ),
    )(part)


def with_meta(tokens, routes, combine):
    flat = routes.reshape(-1)
    index = jnp.arange(flat.shape[0], dtype=jnp.int32)
    same = (flat[:, None] == flat[None, :]) & (index[None, :] < index[:, None])
    rank = jnp.sum(same.astype(jnp.int32), axis=1).reshape(routes.shape)
    high = lax.reduce_precision(combine, 8, 7)
    rest = combine - high
    middle = lax.reduce_precision(rest, 8, 7)
    low = rest - middle
    columns = [routes.astype(F32), rank.astype(F32), high, middle, low]
    meta = jnp.concatenate(columns + [jnp.zeros((ROWS, 128 - 20), F32)], axis=1).astype(BF16)
    pad = jnp.zeros((ROWS, PARTS * PW - 128 - D), BF16)
    wide = jnp.concatenate([tokens, pad, meta], axis=1)
    return wide.reshape(ROWS, PARTS, PW).transpose(1, 0, 2)


def local(tokens, routes, combine, gv, gs, uv, us, dv, ds):
    weights = [w.transpose(1, 0, 2) for w in (gv, gs, uv, us, dv, ds)]
    own_w = dequantize(*weights)
    every, w1, w2 = gather(with_meta(tokens, routes, combine), own_w)
    hidden, place = upward(every, w1)
    partial = downward(hidden, place, w2)
    result = scatter(partial)
    return result.transpose(1, 0, 2).reshape(ROWS, PARTS * PW)[:, :D]


def solution(mesh):
    rows = P(("eg", "tp"), None)
    weight = P("tp", "eg", None)
    return jax.shard_map(
        local,
        mesh=mesh,
        in_specs=(rows, rows, rows) + (weight,) * 6,
        out_specs=rows,
        check_vma=False,
    )
```

time: 772 us -> 1330 us (1.72)
  Pallas kernels: 0 us -> 1320 us
  local copies, waits for them, and re-layouts: 279 us -> 5.14 us
  waiting for transfers between devices: 270 us -> 0 us
  starting transfers between devices: 85.5 us -> 0 us
  blocking collectives: 48.3 us -> 0 us
  other arithmetic: 43.6 us -> 1.56 us
  matrix products: 29.8 us -> 0 us
    pallas_call x0 -> x5, Pallas kernels: none -> 1320 us  [the longest x1 964 us: gather(): pl.pallas_call(gather_kernel, out_shape=[jax.ShapeDtypeStruct((PARTS, 4,...]
    all_to_all x7 -> x0, waiting for transfers between devices: 270 us -> none  [the longest x1 114 us: local(): lax.all_to_all(up_values, 'eg', split_axis=0, concat_axis=1, tiled=True)]
    convert_element_type x13 -> x1, local copies, waits for them, and re-layouts: 201 us -> 0.12 us  [with_meta(): columns = [routes.astype(F32), rank.astype(F32), high, middle, low]]
    all_to_all x7 -> x0, starting transfers between devices: 85.5 us -> none  [the longest x1 31.8 us: local(): lax.all_to_all(up_values, 'eg', split_axis=0, concat_axis=1, tiled=True)]
    all_to_all x1 -> x0, blocking collectives: 48.3 us -> none  [local(): lax.all_to_all(result.reshape(experts, capacity, feature_dim), ('eg', 'tp...]
    convert_element_type x4 -> x0, other arithmetic: 41.6 us -> none  [the longest x2 23.3 us: dequantize(): scaled = shaped.astype(jnp.float32) * scales.astype(jnp.float32)[..., None]]
    unnamed x22 -> x1, local copies, waits for them, and re-layouts: 35.3 us -> 0.78 us
    dot_general x4 -> x0, matrix products: 29.8 us -> none  [the longest x1 19.9 us: expert_ffn(): result = jnp.dot(hidden, w_down, preferred_element_type=jnp.float32)]
  transfers between devices with their start and end apart: 7 -> 0, of which waited for: 6 -> 0; matrix products, arithmetic and copies ran while one was open for 40% -> 0% of each run, Pallas kernels for 0% -> 0%
where the time goes in v1:
time: 1330 us
  Pallas kernels  1320 us (99%)
    pallas_call x1, Pallas kernels, gather(): pl.pallas_call(gather_kernel, out_shape=[jax.ShapeDtypeStruct((PARTS, 4,...  964 us
    pallas_call x1, Pallas kernels, upward(): pl.pallas_call(upward_kernel, grid=(PARTS, EXP // PER_STEP), out_shape=[j...  110 us
    pallas_call x1, Pallas kernels, scatter(): pl.pallas_call(scatter_kernel, out_shape=jax.ShapeDtypeStruct((PARTS, ROW...  100 us
    pallas_call x1, Pallas kernels, dequantize(): pl.pallas_call(dequantize_kernel, grid=(PARTS * PW // width,), out_shape=...  90.1 us
    pallas_call x1, Pallas kernels, downward(): pl.pallas_call(downward_kernel, grid=(PARTS, EXP // PER_STEP), out_shape=...  54 us

profile of v1, /device:TPU:0, one launch (start us, length us, event | category | flops | bytes accessed | tf_op | source)
XLA Modules:
  0.0 1325.3 jit_solution(17991877581282289087)
XLA Ops:
  0.0 0.7 convert_convert_fusion
  0.7 0.7 fusion.1
  1.4 0.1 copy.25
  1.5 0.1 copy.22
  1.6 0.1 copy.24
  1.7 0.1 copy.23
  1.8 0.8 copy.21
  2.6 0.1 eq.15
  2.7 0.2 convert_reduce_fusion
  2.9 0.1 convert_element_type.16
  3.1 1.1 concatenate.6
  4.2 0.8 copy.31
  4.9 90.1 %shard_map.91.own_w = bf16[32,3,48,3072]{3,2,1,0:T(8,128)(2,1)} custom-call(bf16[45,32,2880]{2,1,0:T(8,128)(2,1)} %bitcast.16, bf16[45,32,90]{2,1,0:T(8,128)(2,1)} %bitcast.23, bf16[45,32,2880]{2,1,0:T(8,128)(2,1)} %bitcast.17, bf16[45,32,90]{2,1,0:T(8,128)(2,1)} %bitcast.24, bf16[45,32,2880]{2,1,0:T(8,128)(2,1)} %bitcast.18, bf16[45,32,90]{2,1,0:T(8,128)(2,1)} %bitcast.25), custom_call_target="tpu_custom_call" | custom-call | tf_op jit(solution)/shard_map/pallas_call | solution.py:81
  95.1 964.3 %shard_map.92 = (bf16[3,4,4,4,64,1024]{5,4,3,2,1,0:T(8,128)(2,1)}, bf16[32,256,3072]{2,1,0:T(8,128)(2,1)}, bf16[32,96,3072]{2,1,0:T(8,128)(2,1)}) custom-call(bf16[3,64,1024]{2,1,0:T(8,128)(2,1)} %bitcast.19, bf16[32,3,48,3072]{3,2,1,0:T(8,128)(2,1)} %shard_map.91.own_w), custom_call_target="tpu_custom_call" | custom-call | tf_op jit(solution)/shard_map/pallas_call | solution.py:207
  1059.4 109.9 %shard_map.93 = (bf16[32,256,128]{2,1,0:T(8,128)(2,1)}, bf16[16,256,512]{2,1,0:T(8,128)(2,1)}) custom-call(bf16[3,4,4,4,64,1024]{5,4,3,2,1,0:T(8,128)(2,1)} %get-tuple-element.10.every.meta, bf16[3,4,4,4,64,1024]{5,4,3,2,1,0:T(8,128)(2,1)} %get-tuple-element.10.every.meta, bf16[32,256,3072]{2,1,0:T(8,128)(2,1)} %get-tuple-element.11.w1), custom_call_target="tpu_custom_call" | custom-call | tf_op jit(solution)/shard_map/pallas_call | solution.py:296
  1169.2 54.0 %shard_map.94.part = bf16[3,4,4,4,64,1024]{5,4,3,2,1,0:T(8,128)(2,1)} custom-call(bf16[32,256,128]{2,1,0:T(8,128)(2,1)} %get-tuple-element.12.hidden, bf16[16,256,512]{2,1,0:T(8,128)(2,1)} %get-tuple-element.13.place, bf16[32,96,3072]{2,1,0:T(8,128)(2,1)} %get-tuple-element.14.w2), custom_call_target="tpu_custom_call" | custom-call | tf_op jit(solution)/shard_map/pallas_call | solution.py:341
  1223.2 100.2 %shard_map.95 = bf16[3,64,1024]{2,1,0:T(8,128)(2,1)} custom-call(bf16[3,4,4,4,64,1024]{5,4,3,2,1,0:T(8,128)(2,1)} %shard_map.94.part), custom_call_target="tpu_custom_call" | custom-call | tf_op jit(solution)/shard_map/pallas_call | solution.py:499
  1323.5 1.0 copy.29
  1324.5 0.8 slice.4
  (3 shorter events, 0.0 us)

commit v2 on v1

--- a/solution.py
+++ b/solution.py
@@ -46,69 +46,89 @@
     pl.semaphore_wait(barrier, 7 if sibling else 6)
 
 
-def dequantize_kernel(gv, gs, uv, us, dv, ds, out, flat):
-    step = pl.program_id(0)
-    width = gv.shape[-1]
-    blocks = gs.shape[-1]
-    lane = lax.broadcasted_iota(jnp.int32, (blocks, width), 1) + step * width
-    spread = (lane // BLOCK == lax.broadcasted_iota(jnp.int32, (blocks, width), 0)).astype(BF16)
-    inside = lax.broadcasted_iota(jnp.int32, (EXP, width), 1) + step * width < D
-    for which, (values, scales) in enumerate(((gv, gs), (uv, us), (dv, ds))):
-        def unit(f, _):
-            scale = jnp.dot(scales[f], spread, preferred_element_type=F32)
-            full = jnp.where(inside, values[f].astype(F32) * scale, 0.0)
-            for c in range(width // 128):
-                flat[c, pl.ds(f * EXP, EXP), :] = full[:, c * 128 : (c + 1) * 128]
-            return 0
-
-        lax.fori_loop(0, FS, unit, 0, unroll=5)
+WIDE = 512
+PIECES = 3 * PARTS * PW // WIDE
+PITCH = EXP + 1
+
+
+def gather_kernel(
+    tok, gv, gs, uv, us, dv, ds, every, weights, raw, scales, flat, made, ssem, rsem, lsem, wsem, dsem
+):
+    me, core = position()
+    fetched = []
+    for i, (values, scale) in enumerate(((gv, gs), (uv, us), (dv, ds))):
+        fetched.append(pltpu.make_async_copy(values, raw.at[i], dsem.at[2 * i]))
+        fetched.append(pltpu.make_async_copy(scale, scales.at[i], dsem.at[2 * i + 1]))
+    for c in fetched:
+        c.start()
+    greet(me, core, True)
+
+    def target(n, first):
+        start = pl.multiple_of(n // 3 * WIDE, WIDE)
+        return weights.at[:, n % 3, pl.ds(first, FP), pl.ds(start, WIDE)]
+
+    def keep(n):
+        return pltpu.make_async_copy(made.at[n % 2], target(n, 0), wsem.at[2, n % 2])
+
+    def give(n):
+        return pltpu.make_async_remote_copy(
+            made.at[n % 2],
+            target(n, FP),
+            wsem.at[0, n % 2],
+            wsem.at[1, n],
+            device_id=device(me, 1 - core),
+            device_id_type=MESH,
+        )
+
+    def dequantize(column, which):
+        n = column * 3 + which
+        slot = n % 2
+
+        @pl.when(n >= 2)
+        def _():
+            keep(n - 2).wait()
+            give(n - 2).wait_send()
+
+        start = column * WIDE
+        real = min(WIDE, D - start)
+        blocks = D // BLOCK
+        lane = lax.broadcasted_iota(jnp.int32, (blocks, WIDE), 1) + start
+        spread = (lane // BLOCK == lax.broadcasted_iota(jnp.int32, (blocks, WIDE), 0)).astype(BF16)
+        def units(i, _):
+            count = 5
+            scale = jnp.dot(
+                scales[which, pl.ds(i * count, count)].reshape(count * EXP, blocks),
+                spread,
+                preferred_element_type=F32,
+            )
+            values = raw[which, pl.ds(i * count, count), :, pl.ds(start, real)]
+            full = values.reshape(count * EXP, real).astype(F32) * scale[:, :real]
+            if real < WIDE:
+                full = jnp.concatenate([full, jnp.zeros((count * EXP, WIDE - real), F32)], axis=1)
+            for c in range(WIDE // 128):
+                for k in range(count):
+                    flat[c, pl.ds((i * count + k) * PITCH, EXP), :] = full[
+                        k * EXP : (k + 1) * EXP, c * 128 : (c + 1) * 128
+                    ]
+            return 0
+
+        lax.fori_loop(0, FS // 5, units, 0)
 
         def expert(e, _):
-            rows = jnp.concatenate(
-                [flat[c, pl.ds(e, FS, stride=EXP), :] for c in range(width // 128)], axis=1
-            )
-            rows = jnp.concatenate([rows, jnp.zeros((FP - FS, width), F32)], axis=0)
-            out[e, which] = rows.astype(BF16)
+            for c in range(WIDE // 128):
+                rows = flat[c, pl.ds(e, FS, stride=PITCH), :]
+                rows = jnp.concatenate([rows, jnp.zeros((FP - FS, 128), F32)], axis=0)
+                made[slot, e, :, pl.ds(c * 128, 128)] = rows.astype(BF16)
             return 0
 
         lax.fori_loop(0, EXP, expert, 0, unroll=4)
-
-
-def dequantize(gv, gs, uv, us, dv, ds):
-    width = 512
-    value = pl.BlockSpec((FS, EXP, width), lambda i: (0, 0, i))
-    scale = pl.BlockSpec((FS, EXP, D // BLOCK), lambda i: (0, 0, 0))
-    return pl.pallas_call(
-        dequantize_kernel,
-        grid=(PARTS * PW // width,),
-        out_shape=jax.ShapeDtypeStruct((EXP, 3, FP, PARTS * PW), BF16),
-        in_specs=[value, scale] * 3,
-        out_specs=pl.BlockSpec((EXP, 3, FP, width), lambda i: (0, 0, 0, i)),
-        scratch_shapes=[pltpu.VMEM((width // 128, FS * EXP, 128), F32)],
-        compiler_params=pltpu.CompilerParams(vmem_limit_bytes=VMEM),
-    )(gv, gs, uv, us, dv, ds)
-
-
-def gather_kernel(tok, own_w, every, w1, w2, ssem, rsem, lsem, wsem):
-    me, core = position()
-    greet(me, core, True)
-    pieces = []
-    for i, (source, target, first) in enumerate(((0, w1, 0), (1, w1, 128), (2, w2, 0))):
-        pieces.append(
-            pltpu.make_async_remote_copy(
-                own_w.at[:, source],
-                target.at[:, pl.ds(first + FP, FP)],
-                wsem.at[0, i],
-                wsem.at[1, i],
-                device_id=device(me, 1 - core),
-                device_id_type=MESH,
-            )
-        )
-        pieces.append(
-            pltpu.make_async_copy(own_w.at[:, source], target.at[:, pl.ds(first, FP)], wsem.at[2, i])
-        )
-    for piece in pieces:
-        piece.start()
+        keep(n).start()
+        give(n).start()
+
+    def work(*columns):
+        for column in columns:
+            lax.fori_loop(0, 3, lambda which, _: dequantize(column, which) or 0, 0)
+
     own = [
         pltpu.make_async_copy(tok.at[p], every.at[p, me[0], me[1], me[2]], lsem.at[p])
         for p in range(PARTS)
@@ -161,6 +181,8 @@
     for p in parts:
         for way in ways:
             go(p, 0, 0, way, 0)
+    for c in fetched:
+        c.wait()
     for p in parts:
         for way in ways:
             arrive(p, 0, 0, way, 0)
@@ -189,44 +211,59 @@
         for way in ways:
             go(p, 2, 3, way, 0)
     for jj in range(4):
+        work(*((0, 1), (2,), (3,), (4,))[jj])
         for p in parts:
             for way in ways:
                 arrive(p, 2, jj, way, 0)
                 go(p, 2, jj, way, 1)
+    work(5)
     for jj in range(4):
         for p in parts:
             for way in ways:
                 arrive(p, 2, jj, way, 1)
     for c in sent:
         c.wait_send()
-    for piece in pieces:
-        piece.wait()
-
-
-def gather(tok, own_w):
+    for n in (PIECES - 2, PIECES - 1):
+        keep(n).wait()
+        give(n).wait_send()
+
+    def received(n, _):
+        give(n).wait_recv()
+        return 0
+
+    lax.fori_loop(0, PIECES, received, 0)
+
+
+def gather(tok, *weights):
     return pl.pallas_call(
         gather_kernel,
         out_shape=[
             jax.ShapeDtypeStruct((PARTS, 4, 4, 4, ROWS, PW), BF16),
-            jax.ShapeDtypeStruct((EXP, 256, PARTS * PW), BF16),
-            jax.ShapeDtypeStruct((EXP, 2 * FP, PARTS * PW), BF16),
-        ],
-        in_specs=[ANY] * 2,
-        out_specs=[ANY] * 3,
+            jax.ShapeDtypeStruct((EXP, 3, 2 * FP, PARTS * PW), BF16),
+        ],
+        in_specs=[ANY] * 7,
+        out_specs=[ANY] * 2,
         scratch_shapes=[
+            pltpu.VMEM((3, FS, EXP, D), BF16),
+            pltpu.VMEM((3, FS, EXP, D // BLOCK), BF16),
+            pltpu.VMEM((WIDE // 128, FS * PITCH, 128), F32),
+            pltpu.VMEM((2, EXP, FP, WIDE), BF16),
             pltpu.SemaphoreType.DMA((PARTS, 6, 4)),
             pltpu.SemaphoreType.DMA((PARTS, 6, 4)),
             pltpu.SemaphoreType.DMA((PARTS,)),
-            pltpu.SemaphoreType.DMA((3, 3)),
-        ],
-        compiler_params=pltpu.CompilerParams(collective_id=1, has_side_effects=True),
-    )(tok, own_w)
+            pltpu.SemaphoreType.DMA((3, PIECES)),
+            pltpu.SemaphoreType.DMA((6,)),
+        ],
+        compiler_params=pltpu.CompilerParams(
+            collective_id=1, has_side_effects=True, vmem_limit_bytes=VMEM
+        ),
+    )(tok, *weights)
 
 
 PER_STEP = 4
 
 
-def upward_kernel(every, meta, w1, hidden, place, rows, acc):
+def upward_kernel(every, meta, weights, hidden, place, rows, acc):
     p, step = pl.program_id(0), pl.program_id(1)
     z = lax.axis_index("tp")
 
@@ -237,8 +274,8 @@
         def block(i, _):
             g, b = i // 4, i % 4
             m = meta[0, g // 4, g % 4, b].astype(F32)
-            local = m[:, 0:4] - (z * EXP).astype(F32)
-            ids = local * 16.0 + b.astype(F32) * 4.0 + m[:, 4:8]
+            local = m[:, 64:68] - (z * EXP).astype(F32)
+            ids = local * 16.0 + b.astype(F32) * 4.0 + m[:, 80:84]
             ids = jnp.where((local >= 0.0) & (local < EXP), ids, -1.0)
             hit = slots == ids[:, 0:1]
             for k in range(1, 4):
@@ -247,6 +284,12 @@
             return 0
 
         lax.fori_loop(0, 64, block, 0)
+
+        def clear(e, _):
+            acc[e] = jnp.zeros((256, 256), F32)
+            return 0
+
+        lax.fori_loop(0, EXP, clear, 0)
 
     @pl.when(step == 0)
     def _():
@@ -262,37 +305,30 @@
 
     for i in range(PER_STEP):
         e = step * PER_STEP + i
-        out = lax.dot_general(
-            rows[e], w1[i], (((1,), (1,)), ((), ())), preferred_element_type=F32
+        acc[e, :, pl.ds(0, 4 * FP)] += lax.dot_general(
+            rows[e],
+            weights[i].reshape(4 * FP, PW),
+            (((1,), (1,)), ((), ())),
+            preferred_element_type=F32,
         )
 
-        @pl.when(p == 0)
-        def _():
-            acc[e] = out
-
-        @pl.when(p == 1)
-        def _():
-            acc[e] += out
-
-        @pl.when(p == 2)
-        def _():
-            total = acc[e] + out
-            gate, up = total[:, :128], total[:, 128:]
-            made = gate / (1.0 + jnp.exp(-gate)) * up
+    @pl.when(p == PARTS - 1)
+    def _():
+        ones = jnp.ones((128, 128), BF16)
+        lane = lax.broadcasted_iota(jnp.int32, (256, 128), 1)
+        for i in range(PER_STEP):
+            e = step * PER_STEP + i
+            total = acc[e]
+            gate, up = total[:, :128], pltpu.roll(total, 128 - 2 * FP, 1)[:, 128:]
             m = rows[e, :, META:].astype(F32)
-            named = (m[:, 0:4] == (z * EXP + e).astype(F32)).astype(F32)
-            weights = [
-                jnp.sum(m[:, 8 + 4 * i : 12 + 4 * i] * named, axis=1, keepdims=True)
-                for i in range(3)
-            ]
-            lane = lax.broadcasted_iota(jnp.int32, made.shape, 1)
-            for i in range(3):
-                made = jnp.where(lane == 96 + i, weights[i], made)
-            made = jnp.where(lane > 98, 0.0, made)
-            hidden[e] = made.astype(BF16)
-
-
-def upward(every, w1):
+            named = pltpu.roll(m, 64, 1) == (z * EXP + e).astype(F32)
+            chosen = jnp.where(named & (lane < 12), m, 0.0).astype(BF16)
+            weight = jnp.dot(chosen, ones, preferred_element_type=F32)
+            value = gate / (1.0 + jnp.exp(-gate)) * up * weight
+            hidden[e] = value.astype(BF16)
+
+
+def upward(every, weights):
     return pl.pallas_call(
         upward_kernel,
         grid=(PARTS, EXP // PER_STEP),
@@ -303,7 +339,7 @@
         in_specs=[
             pl.BlockSpec((1, 4, 4, 4, ROWS, PW), lambda p, s: (p, 0, 0, 0, 0, 0)),
             pl.BlockSpec((1, 4, 4, 4, ROWS, 128), lambda p, s: (2, 0, 0, 0, 0, 7)),
-            pl.BlockSpec((PER_STEP, 256, PW), lambda p, s: (s, 0, p)),
+            pl.BlockSpec((PER_STEP, 2, 2 * FP, PW), lambda p, s: (s, 0, 0, p)),
         ],
         out_specs=[
             pl.BlockSpec((EXP, 256, 128), lambda p, s: (0, 0, 0)),
@@ -314,17 +350,14 @@
             pltpu.VMEM((EXP, 256, 256), F32),
         ],
         compiler_params=pltpu.CompilerParams(vmem_limit_bytes=VMEM),
-    )(every, every, w1)
+    )(every, every, weights)
 
 
 def downward_kernel(hidden, place, w2, out, results):
     step = pl.program_id(1)
     for i in range(PER_STEP):
         e = step * PER_STEP + i
-        h = hidden[e]
-        w = h[:, 96:99].astype(F32)
-        w = (w[:, 0:1] + w[:, 1:2]) + w[:, 2:3]
-        y = jnp.dot(h[:, : 2 * FP], w2[i], preferred_element_type=F32) * w
+        y = jnp.dot(hidden[e, :, : 2 * FP], w2[i, 0], preferred_element_type=F32)
         results[:, pl.ds(e * 16, 16), :] = y.astype(BF16).reshape(16, 16, PW)
 
     @pl.when(step == EXP // PER_STEP - 1)
@@ -345,7 +378,7 @@
         in_specs=[
             pl.BlockSpec((EXP, 256, 128), lambda p, s: (0, 0, 0)),
             pl.BlockSpec((16, 4 * ROWS, EXP * 16), lambda p, s: (0, 0, 0)),
-            pl.BlockSpec((PER_STEP, 2 * FP, PW), lambda p, s: (s, 0, p)),
+            pl.BlockSpec((PER_STEP, 1, 2 * FP, PW), lambda p, s: (s, 2, 0, p)),
         ],
         out_specs=pl.BlockSpec((1, 4, 4, 4, ROWS, PW), lambda p, s: (p, 0, 0, 0, 0, 0)),
         scratch_shapes=[pltpu.VMEM((16, EXP * 16, PW), BF16)],
@@ -529,8 +562,10 @@
     rest = combine - high
     middle = lax.reduce_precision(rest, 8, 7)
     low = rest - middle
-    columns = [routes.astype(F32), rank.astype(F32), high, middle, low]
-    meta = jnp.concatenate(columns + [jnp.zeros((ROWS, 128 - 20), F32)], axis=1).astype(BF16)
+    named = routes.astype(F32)
+    columns = [high, middle, low, jnp.zeros((ROWS, 52), F32), named, named, named]
+    columns += [jnp.zeros((ROWS, 4), F32), rank.astype(F32), jnp.zeros((ROWS, 44), F32)]
+    meta = jnp.concatenate(columns, axis=1).astype(BF16)
     pad = jnp.zeros((ROWS, PARTS * PW - 128 - D), BF16)
     wide = jnp.concatenate([tokens, pad, meta], axis=1)
     return wide.reshape(ROWS, PARTS, PW).transpose(1, 0, 2)
@@ -538,10 +573,9 @@
 
 def local(tokens, routes, combine, gv, gs, uv, us, dv, ds):
     weights = [w.transpose(1, 0, 2) for w in (gv, gs, uv, us, dv, ds)]
-    own_w = dequantize(*weights)
-    every, w1, w2 = gather(with_meta(tokens, routes, combine), own_w)
-    hidden, place = upward(every, w1)
-    partial = downward(hidden, place, w2)
+    every, ready = gather(with_meta(tokens, routes, combine), *weights)
+    hidden, place = upward(every, ready)
+    partial = downward(hidden, place, ready)
     result = scatter(partial)
     return result.transpose(1, 0, 2).reshape(ROWS, PARTS * PW)[:, :D]
 

time: 1330 us -> 346 us (0.26)
  Pallas kernels: 1320 us -> 338 us
    pallas_call x1, Pallas kernels: 964 us -> 107 us  [gather(): pl.pallas_call(gather_kernel, out_shape=[jax.ShapeDtypeStruct((PARTS, 4,...]
    pallas_call x1 -> x0, Pallas kernels: 90.1 us -> none  [dequantize(): pl.pallas_call(dequantize_kernel, grid=(PARTS * PW // width,), out_shape=...]
    pallas_call x1, Pallas kernels: 110 us -> 76.4 us  [upward(): pl.pallas_call(upward_kernel, grid=(PARTS, EXP // PER_STEP), out_shape=[j...]
where the time goes in v2:
time: 346 us; the launch traced here: 345 us
  Pallas kernels  338 us (98%)
  local copies, waits for them, and re-layouts  5.18 us (1%)
    pallas_call x1, Pallas kernels, gather(): pl.pallas_call(gather_kernel, out_shape=[jax.ShapeDtypeStruct((PARTS, 4,...  107 us
    pallas_call x1, Pallas kernels, scatter(): pl.pallas_call(scatter_kernel, out_shape=jax.ShapeDtypeStruct((PARTS, ROW...  100 us
    pallas_call x1, Pallas kernels, upward(): pl.pallas_call(upward_kernel, grid=(PARTS, EXP // PER_STEP), out_shape=[j...  76.4 us
    pallas_call x1, Pallas kernels, downward(): pl.pallas_call(downward_kernel, grid=(PARTS, EXP // PER_STEP), out_shape=...  54.4 us

profile of v2, /device:TPU:0, one launch (start us, length us, event | category | flops | bytes accessed | tf_op | source)
XLA Modules:
  0.0 344.9 jit_solution(11562976954799789007)
XLA Ops:
  0.0 0.7 convert_convert_fusion
  0.7 0.7 fusion.1
  1.4 0.1 copy.28
  1.5 0.1 copy.29
  1.6 0.1 copy.27
  1.7 0.1 copy.26
  1.8 0.8 copy.25
  2.6 0.1 eq.15
  2.7 0.2 convert_reduce_fusion
  2.9 0.1 convert_element_type.16
  3.1 1.1 concatenate.6
  4.2 0.8 copy.37
  5.0 107.2 %shard_map.91 = (bf16[3,4,4,4,64,1024]{5,4,3,2,1,0:T(8,128)(2,1)}, bf16[32,3,96,3072]{3,2,1,0:T(8,128)(2,1)}) custom-call(bf16[3,64,1024]{2,1,0:T(8,128)(2,1)} %bitcast.20, bf16[45,32,2880]{2,1,0:T(8,128)(2,1)} %bitcast.16, bf16[45,32,90]{2,1,0:T(8,128)(2,1)} %bitcast.23, bf16[45,32,2880]{2,1,0:T(8,128)(2,1)} %bitcast.17, bf16[45,32,90]{2,1,0:T(8,128)(2,1)} %bitcast.24, ...), custom_call_target="tpu_custom_call" | custom-call | tf_op jit(solution)/shard_map/pallas_call | solution.py:238
  112.2 76.4 %shard_map.92 = (bf16[32,256,128]{2,1,0:T(8,128)(2,1)}, bf16[16,256,512]{2,1,0:T(8,128)(2,1)}) custom-call(bf16[3,4,4,4,64,1024]{5,4,3,2,1,0:T(8,128)(2,1)} %get-tuple-element.9.every.meta, bf16[3,4,4,4,64,1024]{5,4,3,2,1,0:T(8,128)(2,1)} %get-tuple-element.9.every.meta, bf16[32,3,96,3072]{3,2,1,0:T(8,128)(2,1)} %get-tuple-element.10.weights.w2), custom_call_target="tpu_custom_call" | custom-call | tf_op jit(solution)/shard_map/pallas_call | solution.py:332
  188.6 54.4 %shard_map.93.part = bf16[3,4,4,4,64,1024]{5,4,3,2,1,0:T(8,128)(2,1)} custom-call(bf16[32,256,128]{2,1,0:T(8,128)(2,1)} %get-tuple-element.11.hidden, bf16[16,256,512]{2,1,0:T(8,128)(2,1)} %get-tuple-element.12.place, bf16[32,3,96,3072]{3,2,1,0:T(8,128)(2,1)} %get-tuple-element.10.weights.w2), custom_call_target="tpu_custom_call" | custom-call | tf_op jit(solution)/shard_map/pallas_call | solution.py:374
  243.0 100.1 %shard_map.94 = bf16[3,64,1024]{2,1,0:T(8,128)(2,1)} custom-call(bf16[3,4,4,4,64,1024]{5,4,3,2,1,0:T(8,128)(2,1)} %shard_map.93.part), custom_call_target="tpu_custom_call" | custom-call | tf_op jit(solution)/shard_map/pallas_call | solution.py:532
  343.1 1.0 copy.35
  344.2 0.8 slice.4
  (5 shorter events, 0.0 us)

commit v3 on v2

--- a/solution.py
+++ b/solution.py
@@ -353,51 +353,83 @@
     )(every, every, weights)
 
 
-def downward_kernel(hidden, place, w2, out, results):
-    step = pl.program_id(1)
-    for i in range(PER_STEP):
-        e = step * PER_STEP + i
-        y = jnp.dot(hidden[e, :, : 2 * FP], w2[i, 0], preferred_element_type=F32)
-        results[:, pl.ds(e * 16, 16), :] = y.astype(BF16).reshape(16, 16, PW)
-
-    @pl.when(step == EXP // PER_STEP - 1)
-    def _():
-        def group(g, _):
-            summed = jnp.dot(place[g], results[g], preferred_element_type=F32)
-            out[0, g // 4, g % 4] = summed.astype(BF16).reshape(4, ROWS, PW)
-            return 0
-
-        lax.fori_loop(0, 16, group, 0)
-
-
-def downward(hidden, place, w2):
-    return pl.pallas_call(
-        downward_kernel,
-        grid=(PARTS, EXP // PER_STEP),
-        out_shape=jax.ShapeDtypeStruct((PARTS, 4, 4, 4, ROWS, PW), BF16),
-        in_specs=[
-            pl.BlockSpec((EXP, 256, 128), lambda p, s: (0, 0, 0)),
-            pl.BlockSpec((16, 4 * ROWS, EXP * 16), lambda p, s: (0, 0, 0)),
-            pl.BlockSpec((PER_STEP, 1, 2 * FP, PW), lambda p, s: (s, 2, 0, p)),
-        ],
-        out_specs=pl.BlockSpec((1, 4, 4, 4, ROWS, PW), lambda p, s: (p, 0, 0, 0, 0, 0)),
-        scratch_shapes=[pltpu.VMEM((16, EXP * 16, PW), BF16)],
-        compiler_params=pltpu.CompilerParams(vmem_limit_bytes=VMEM),
-    )(hidden, place, w2)
-
-
-def scatter_kernel(part, out, far0, near0, mid0, acc, far1, near1, far2, near2, own2, sems, lsem):
+CHUNKS = 2
+CW = PW // CHUNKS
+BATCH = 8
+BATCHES = EXP // BATCH
+STAGES = 8
+
+
+def downward_kernel(
+    hidden, place, weights, out, part,
+    far0, near0, mid0, acc, far1, near1, far2, near2, own2,
+    results, stage, wbuf, sems, lsem, wsem, psem,
+):
     me, core = position()
-    greet(me, core, False)
     parts = range(PARTS)
     sent = []
 
-    def copy(here, there, p, phase, jj, kind, way, axis):
+    def fetch(n):
+        unit = n // BATCHES
+        start = pl.multiple_of(unit % PARTS * PW + unit // PARTS * CW, CW)
+        first = n % BATCHES * BATCH
+        return pltpu.make_async_copy(
+            weights.at[pl.ds(first, BATCH), 2, :, pl.ds(start, CW)], wbuf.at[n % 2], wsem.at[n % 2]
+        )
+
+    fetch(0).start()
+    greet(me, core, False)
+
+    def experts(c, p):
+        def batch(s, _):
+            n = (c * PARTS + p) * BATCHES + s
+            fetch(n).wait()
+
+            @pl.when(n + 1 < CHUNKS * PARTS * BATCHES)
+            def _():
+                fetch(n + 1).start()
+
+            for i in range(BATCH):
+                e = s * BATCH + i
+                y = jnp.dot(
+                    hidden[e, :, : 2 * FP], wbuf[n % 2, i], preferred_element_type=F32
+                )
+                first = pl.multiple_of(e * 16, 16)
+                results[:, pl.ds(first, 16), :] = y.astype(BF16).reshape(16, 16, CW)
+            return 0
+
+        lax.fori_loop(0, BATCHES, batch, 0)
+
+    def combine(c, p):
+        def store(g):
+            return pltpu.make_async_copy(
+                stage.at[g % STAGES], part.at[c, p, g // 4, g % 4], psem.at[g % STAGES]
+            )
+
+        def group(g, _):
+            @pl.when(g >= STAGES)
+            def _():
+                store(g - STAGES).wait()
+
+            summed = jnp.dot(place[g], results[g], preferred_element_type=F32)
+            stage[g % STAGES] = summed.astype(BF16).reshape(4, ROWS, CW)
+            store(g).start()
+            return 0
+
+        lax.fori_loop(0, 16, group, 0, unroll=2)
+
+        def stored(g, _):
+            store(g).wait()
+            return 0
+
+        lax.fori_loop(16 - STAGES, 16, stored, 0)
+
+    def copy(here, there, c, p, phase, kind, way, axis):
         return pltpu.make_async_remote_copy(
             here,
             there,
-            sems.at[0, p, phase + jj, kind],
-            sems.at[1, p, phase + jj, kind],
+            sems.at[0, c, p, phase, kind],
+            sems.at[1, c, p, phase, kind],
             device_id=device(moved(me, axis, way), core),
             device_id_type=MESH,
         )
@@ -407,41 +439,36 @@
         c.start()
         sent.append(c)
 
-    def j_of(p, jj):
-        return (me[(p + 1) % 3] + (2, 1, -1, 0)[jj] + 4) % 4
-
-    def piece(p, jj, by, rows):
-        o0, o1, o2 = p, (p + 1) % 3, (p + 2) % 3
+    def wait_in(there, c, p, phase, kind, axis):
+        copy(there, there, c, p, phase, kind, 1, axis).wait_recv()
+
+    top, bottom, whole = pl.ds(0, 32), pl.ds(32, 32), slice(None)
+
+    def piece(c, p, jj, by, rows):
+        o1, o2 = (p + 1) % 3, (p + 2) % 3
         index = [slice(None)] * 3
-        index[o1] = j_of(p, jj)
+        index[o1] = (me[o1] + (2, 1, -1, 0)[jj] + 4) % 4
         index[o2] = (me[o2] + by + 4) % 4
-        return part.at[(p, *index, rows)]
-
-    top, bottom, whole = pl.ds(0, 32), pl.ds(32, 32), slice(None)
-
-    def load(p, jj, k):
+        return part.at[(c, p, *index, rows)]
+
+    def load(c, p, jj, k):
         by, rows = ((1, top), (-1, bottom), (0, whole))[k]
-        there = acc.at[p, jj] if k == 2 else mid0.at[p, jj, k]
-        return pltpu.make_async_copy(piece(p, jj, by, rows), there, lsem.at[p, jj, k])
-
-    def issue(jj):
-        for p in parts:
+        there = acc.at[c, p, jj] if k == 2 else mid0.at[c, p, jj, k]
+        return pltpu.make_async_copy(piece(c, p, jj, by, rows), there, lsem.at[c, p, jj, k])
+
+    def issue(c, jj, which=parts):
+        for p in which:
             axis = (p + 2) % 3
-            go(piece(p, jj, 2, top), far0.at[p, jj, 0], p, 0, jj, 0, 1, axis)
-            go(piece(p, jj, 2, bottom), far0.at[p, jj, 1], p, 0, jj, 1, -1, axis)
+            go(piece(c, p, jj, 2, top), far0.at[c, p, jj, 0], c, p, jj, 0, 1, axis)
+            go(piece(c, p, jj, 2, bottom), far0.at[c, p, jj, 1], c, p, jj, 1, -1, axis)
             for k in range(3):
-                load(p, jj, k).start()
-        for p in parts:
+                load(c, p, jj, k).start()
+        for p in which:
             axis = (p + 2) % 3
-            go(piece(p, jj, 1, bottom), near0.at[p, jj, 0, :, bottom], p, 0, jj, 2, 1, axis)
-            go(piece(p, jj, -1, top), near0.at[p, jj, 1, :, top], p, 0, jj, 3, -1, axis)
-
-    def wait_in(there, p, phase, jj, kind, axis):
-        copy(there, there, p, phase, jj, kind, 1, axis).wait_recv()
+            go(piece(c, p, jj, 1, bottom), near0.at[c, p, jj, 0, :, bottom], c, p, jj, 2, 1, axis)
+            go(piece(c, p, jj, -1, top), near0.at[c, p, jj, 1, :, top], c, p, jj, 3, -1, axis)
 
     def add(target, *others):
-        count = target.shape[0]
-
         def one(i, _):
             total = target[i].astype(F32)
             for other in others:
@@ -449,108 +476,153 @@
             target[i] = total.astype(BF16)
             return 0
 
-        lax.fori_loop(0, count, one, 0)
-
-    def middle(jj):
+        lax.fori_loop(0, target.shape[0], one, 0)
+
+    def middle(c, jj):
         for p in parts:
             axis = (p + 2) % 3
             for k, way in ((0, 1), (1, -1)):
                 half = top if k == 0 else bottom
-                load(p, jj, k).wait()
-                wait_in(far0.at[p, jj, k], p, 0, jj, k, axis)
-                add(mid0.at[p, jj, k], far0.at[p, jj, k])
-                go(mid0.at[p, jj, k], near0.at[p, jj, k, :, half], p, 0, jj, 4 + k, way, axis)
-
-    def finish(jj):
+                load(c, p, jj, k).wait()
+                wait_in(far0.at[c, p, jj, k], c, p, jj, k, axis)
+                add(mid0.at[c, p, jj, k], far0.at[c, p, jj, k])
+                go(mid0.at[c, p, jj, k], near0.at[c, p, jj, k, :, half], c, p, jj, 4 + k, way, axis)
+
+    def collect(near, c, p, phase, axis, lead):
+        for kind, k, half in ((2, 0, bottom), (3, 1, top), (4, 0, top), (5, 1, bottom)):
+            wait_in(near.at[(*lead, k, *([whole] if phase < 5 else []), half)], c, p, phase, kind, axis)
+
+    def finish(c, jj):
         for p in parts:
-            axis = (p + 2) % 3
-            load(p, jj, 2).wait()
-            wait_in(near0.at[p, jj, 0, :, bottom], p, 0, jj, 2, axis)
-            wait_in(near0.at[p, jj, 1, :, top], p, 0, jj, 3, axis)
-            wait_in(near0.at[p, jj, 0, :, top], p, 0, jj, 4, axis)
-            wait_in(near0.at[p, jj, 1, :, bottom], p, 0, jj, 5, axis)
-            add(acc.at[p, jj], near0.at[p, jj, 0], near0.at[p, jj, 1])
+            load(c, p, jj, 2).wait()
+            collect(near0, c, p, jj, (p + 2) % 3, (c, p, jj))
+            add(acc.at[c, p, jj], near0.at[c, p, jj, 0], near0.at[c, p, jj, 1])
             axis = (p + 1) % 3
             if jj == 0:
-                go(acc.at[p, 0, :, top], far1.at[p, 0], p, 4, 0, 0, 1, axis)
-                go(acc.at[p, 0, :, bottom], far1.at[p, 1], p, 4, 0, 1, -1, axis)
+                go(acc.at[c, p, 0, :, top], far1.at[c, p, 0], c, p, 4, 0, 1, axis)
+                go(acc.at[c, p, 0, :, bottom], far1.at[c, p, 1], c, p, 4, 1, -1, axis)
             elif jj == 1:
-                go(acc.at[p, 1, :, bottom], near1.at[p, 0, :, bottom], p, 4, 0, 2, 1, axis)
+                go(acc.at[c, p, 1, :, bottom], near1.at[c, p, 0, :, bottom], c, p, 4, 2, 1, axis)
             elif jj == 2:
-                go(acc.at[p, 2, :, top], near1.at[p, 1, :, top], p, 4, 0, 3, -1, axis)
+                go(acc.at[c, p, 2, :, top], near1.at[c, p, 1, :, top], c, p, 4, 3, -1, axis)
         if jj in (1, 2):
             k, way, half = (0, 1, top) if jj == 1 else (1, -1, bottom)
             for p in parts:
                 axis = (p + 1) % 3
-                wait_in(far1.at[p, k], p, 4, 0, k, axis)
-                add(acc.at[p, jj, :, half], far1.at[p, k])
-                go(acc.at[p, jj, :, half], near1.at[p, k, :, half], p, 4, 0, 4 + k, way, axis)
-
-    issue(0)
-    issue(1)
-    for jj in range(4):
-        middle(jj)
-        if jj + 2 < 4:
-            issue(jj + 2)
-        if jj >= 1:
-            finish(jj - 1)
-    finish(3)
-    for p in parts:
-        axis = (p + 1) % 3
-        wait_in(near1.at[p, 0, :, bottom], p, 4, 0, 2, axis)
-        wait_in(near1.at[p, 1, :, top], p, 4, 0, 3, axis)
-        wait_in(near1.at[p, 0, :, top], p, 4, 0, 4, axis)
-        wait_in(near1.at[p, 1, :, bottom], p, 4, 0, 5, axis)
-        add(acc.at[p, 3], near1.at[p, 0], near1.at[p, 1])
-        t = [(me[p] + by + 4) % 4 for by in (2, 1, -1, 0)]
-        go(acc.at[p, 3, t[0], top], far2.at[p, 0], p, 5, 0, 0, 1, p)
-        go(acc.at[p, 3, t[0], bottom], far2.at[p, 1], p, 5, 0, 1, -1, p)
-        go(acc.at[p, 3, t[1], bottom], near2.at[p, 0, bottom], p, 5, 0, 2, 1, p)
-        go(acc.at[p, 3, t[2], top], near2.at[p, 1, top], p, 5, 0, 3, -1, p)
-    for p in parts:
-        t = [(me[p] + by + 4) % 4 for by in (2, 1, -1, 0)]
-        for k, way, half in ((0, 1, top), (1, -1, bottom)):
-            wait_in(far2.at[p, k], p, 5, 0, k, p)
-            own2[p, k] = (
-                acc[p, 3, t[1 + k], half].astype(F32) + far2[p, k].astype(F32)
+                wait_in(far1.at[c, p, k], c, p, 4, k, axis)
+                add(acc.at[c, p, jj, :, half], far1.at[c, p, k])
+                go(acc.at[c, p, jj, :, half], near1.at[c, p, k, :, half], c, p, 4, 4 + k, way, axis)
+
+    def lines(p):
+        return [(me[p] + by + 4) % 4 for by in (2, 1, -1, 0)]
+
+    def last_start(c):
+        for p in parts:
+            collect(near1, c, p, 4, (p + 1) % 3, (c, p))
+            add(acc.at[c, p, 3], near1.at[c, p, 0], near1.at[c, p, 1])
+            t = lines(p)
+            go(acc.at[c, p, 3, t[0], top], far2.at[c, p, 0], c, p, 5, 0, 1, p)
+            go(acc.at[c, p, 3, t[0], bottom], far2.at[c, p, 1], c, p, 5, 1, -1, p)
+            go(acc.at[c, p, 3, t[1], bottom], near2.at[c, p, 0, bottom], c, p, 5, 2, 1, p)
+            go(acc.at[c, p, 3, t[2], top], near2.at[c, p, 1, top], c, p, 5, 3, -1, p)
+
+    def last_middle(c):
+        for p in parts:
+            t = lines(p)
+            for k, way, half in ((0, 1, top), (1, -1, bottom)):
+                wait_in(far2.at[c, p, k], c, p, 5, k, p)
+                own2[c, p, k] = (
+                    acc[c, p, 3, t[1 + k], half].astype(F32) + far2[c, p, k].astype(F32)
+                ).astype(BF16)
+                go(own2.at[c, p, k], near2.at[c, p, k, half], c, p, 5, 4 + k, way, p)
+
+    def last_finish(c):
+        for p in parts:
+            collect(near2, c, p, 5, p, (c, p))
+            out[c, p] = (
+                acc[c, p, 3, me[p]].astype(F32)
+                + near2[c, p, 0].astype(F32)
+                + near2[c, p, 1].astype(F32)
             ).astype(BF16)
-            go(own2.at[p, k], near2.at[p, k, half], p, 5, 0, 4 + k, way, p)
-    for p in parts:
-        wait_in(near2.at[p, 0, bottom], p, 5, 0, 2, p)
-        wait_in(near2.at[p, 1, top], p, 5, 0, 3, p)
-        wait_in(near2.at[p, 0, top], p, 5, 0, 4, p)
-        wait_in(near2.at[p, 1, bottom], p, 5, 0, 5, p)
-        out[p] = (
-            acc[p, 3, me[p]].astype(F32) + near2[p, 0].astype(F32) + near2[p, 1].astype(F32)
-        ).astype(BF16)
+
+    for p in parts:
+        experts(0, p)
+        combine(0, p)
+        issue(0, 0, (p,))
+        issue(0, 1, (p,))
+    experts(1, 0)
+    middle(0, 0)
+    issue(0, 2)
+    combine(1, 0)
+    issue(1, 0, (0,))
+    middle(0, 1)
+    issue(0, 3)
+    experts(1, 1)
+    finish(0, 0)
+    combine(1, 1)
+    issue(1, 0, (1,))
+    middle(0, 2)
+    experts(1, 2)
+    finish(0, 1)
+    middle(0, 3)
+    combine(1, 2)
+    issue(1, 0, (2,))
+    issue(1, 1)
+    finish(0, 2)
+    finish(0, 3)
+    middle(1, 0)
+    issue(1, 2)
+    last_start(0)
+    middle(1, 1)
+    issue(1, 3)
+    last_middle(0)
+    finish(1, 0)
+    middle(1, 2)
+    finish(1, 1)
+    last_finish(0)
+    middle(1, 3)
+    finish(1, 2)
+    finish(1, 3)
+    last_start(1)
+    last_middle(1)
+    last_finish(1)
     for c in sent:
         c.wait_send()
 
 
-def scatter(part):
+def downward(hidden, place, weights):
     half = ROWS // 2
+    vmem = pl.BlockSpec(memory_space=pltpu.VMEM)
     return pl.pallas_call(
-        scatter_kernel,
-        out_shape=jax.ShapeDtypeStruct((PARTS, ROWS, PW), BF16),
-        in_specs=[ANY],
-        out_specs=pl.BlockSpec(memory_space=pltpu.VMEM),
+        downward_kernel,
+        out_shape=[
+            jax.ShapeDtypeStruct((CHUNKS, PARTS, ROWS, CW), BF16),
+            jax.ShapeDtypeStruct((CHUNKS, PARTS, 4, 4, 4, ROWS, CW), BF16),
+        ],
+        in_specs=[vmem, vmem, ANY],
+        out_specs=[vmem, ANY],
         scratch_shapes=[
-            pltpu.VMEM((PARTS, 4, 2, 4, half, PW), BF16),
-            pltpu.VMEM((PARTS, 4, 2, 4, ROWS, PW), BF16),
-            pltpu.VMEM((PARTS, 4, 2, 4, half, PW), BF16),
-            pltpu.VMEM((PARTS, 4, 4, ROWS, PW), BF16),
-            pltpu.VMEM((PARTS, 2, 4, half, PW), BF16),
-            pltpu.VMEM((PARTS, 2, 4, ROWS, PW), BF16),
-            pltpu.VMEM((PARTS, 2, half, PW), BF16),
-            pltpu.VMEM((PARTS, 2, ROWS, PW), BF16),
-            pltpu.VMEM((PARTS, 2, half, PW), BF16),
-            pltpu.SemaphoreType.DMA((2, PARTS, 6, 6)),
-            pltpu.SemaphoreType.DMA((PARTS, 4, 3)),
+            pltpu.VMEM((CHUNKS, PARTS, 4, 2, 4, half, CW), BF16),
+            pltpu.VMEM((CHUNKS, PARTS, 4, 2, 4, ROWS, CW), BF16),
+            pltpu.VMEM((CHUNKS, PARTS, 4, 2, 4, half, CW), BF16),
+            pltpu.VMEM((CHUNKS, PARTS, 4, 4, ROWS, CW), BF16),
+            pltpu.VMEM((CHUNKS, PARTS, 2, 4, half, CW), BF16),
+            pltpu.VMEM((CHUNKS, PARTS, 2, 4, ROWS, CW), BF16),
+            pltpu.VMEM((CHUNKS, PARTS, 2, half, CW), BF16),
+            pltpu.VMEM((CHUNKS, PARTS, 2, ROWS, CW), BF16),
+            pltpu.VMEM((CHUNKS, PARTS, 2, half, CW), BF16),
+            pltpu.VMEM((16, EXP * 16, CW), BF16),
+            pltpu.VMEM((STAGES, 4, ROWS, CW), BF16),
+            pltpu.VMEM((2, BATCH, 2 * FP, CW), BF16),
+            pltpu.SemaphoreType.DMA((2, CHUNKS, PARTS, 6, 6)),
+            pltpu.SemaphoreType.DMA((CHUNKS, PARTS, 4, 3)),
+            pltpu.SemaphoreType.DMA((2,)),
+            pltpu.SemaphoreType.DMA((STAGES,)),
         ],
         compiler_params=pltpu.CompilerParams(
             collective_id=2, has_side_effects=True, vmem_limit_bytes=VMEM
         ),
-    )(part)
+    )(hidden, place, weights)
 
 
 def with_meta(tokens, routes, combine):
@@ -575,9 +647,8 @@
     weights = [w.transpose(1, 0, 2) for w in (gv, gs, uv, us, dv, ds)]
     every, ready = gather(with_meta(tokens, routes, combine), *weights)
     hidden, place = upward(every, ready)
-    partial = downward(hidden, place, ready)
-    result = scatter(partial)
-    return result.transpose(1, 0, 2).reshape(ROWS, PARTS * PW)[:, :D]
+    result = downward(hidden, place, ready)[0]
+    return result.transpose(2, 1, 0, 3).reshape(ROWS, PARTS * PW)[:, :D]
 
 
 def solution(mesh):

time: 346 us -> 331 us (0.957)
  Pallas kernels: 338 us -> 322 us
    pallas_call x2 -> x1, Pallas kernels: 155 us -> 138 us  [downward(): pl.pallas_call(downward_kernel, out_shape=[jax.ShapeDtypeStruct((CHUNKS,...]
where the time goes in v3:
time: 331 us; the launch traced here: 329 us
  Pallas kernels  322 us (97%)
  local copies, waits for them, and re-layouts  5.83 us (2%)
    pallas_call x1, Pallas kernels, downward(): pl.pallas_call(downward_kernel, out_shape=[jax.ShapeDtypeStruct((CHUNKS,...  138 us
    pallas_call x1, Pallas kernels, gather(): pl.pallas_call(gather_kernel, out_shape=[jax.ShapeDtypeStruct((PARTS, 4,...  107 us
    pallas_call x1, Pallas kernels, upward(): pl.pallas_call(upward_kernel, grid=(PARTS, EXP // PER_STEP), out_shape=[j...  76.3 us

profile of v3, /device:TPU:0, one launch (start us, length us, event | category | flops | bytes accessed | tf_op | source)
XLA Modules:
  0.0 329.2 jit_solution(8280331739960654041)
XLA Ops:
  0.0 0.7 convert_convert_fusion
  0.7 0.7 fusion.1
  1.4 0.1 copy.28
  1.5 0.1 copy.29
  1.6 0.1 copy.27
  1.7 0.1 copy.26
  1.8 0.8 copy.25
  2.6 0.1 eq.15
  2.7 0.2 convert_reduce_fusion
  2.9 0.1 convert_element_type.16
  3.1 1.1 concatenate.6
  4.2 0.8 copy.36
  5.0 107.2 %shard_map.91 = (bf16[3,4,4,4,64,1024]{5,4,3,2,1,0:T(8,128)(2,1)}, bf16[32,3,96,3072]{3,2,1,0:T(8,128)(2,1)}) custom-call(bf16[3,64,1024]{2,1,0:T(8,128)(2,1)} %bitcast.18, bf16[45,32,2880]{2,1,0:T(8,128)(2,1)} %bitcast.14, bf16[45,32,90]{2,1,0:T(8,128)(2,1)} %bitcast.20, bf16[45,32,2880]{2,1,0:T(8,128)(2,1)} %bitcast.15, bf16[45,32,90]{2,1,0:T(8,128)(2,1)} %bitcast.21, ...), custom_call_target="tpu_custom_call" | custom-call | tf_op jit(solution)/shard_map/pallas_call | solution.py:238
  112.2 76.3 %shard_map.92 = (bf16[32,256,128]{2,1,0:T(8,128)(2,1)}, bf16[16,256,512]{2,1,0:T(8,128)(2,1)}) custom-call(bf16[3,4,4,4,64,1024]{5,4,3,2,1,0:T(8,128)(2,1)} %get-tuple-element.10.every.meta, bf16[3,4,4,4,64,1024]{5,4,3,2,1,0:T(8,128)(2,1)} %get-tuple-element.10.every.meta, bf16[32,3,96,3072]{3,2,1,0:T(8,128)(2,1)} %get-tuple-element.11.weights), custom_call_target="tpu_custom_call" | custom-call | tf_op jit(solution)/shard_map/pallas_call | solution.py:332
  188.6 138.2 %shard_map.93 = (bf16[2,3,64,512]{3,2,1,0:T(8,128)(2,1)}, bf16[2,3,4,4,4,64,512]{6,5,4,3,2,1,0:T(8,128)(2,1)}) custom-call(bf16[32,256,128]{2,1,0:T(8,128)(2,1)} %get-tuple-element.12.hidden, bf16[16,256,512]{2,1,0:T(8,128)(2,1)} %get-tuple-element.13.place, bf16[32,3,96,3072]{3,2,1,0:T(8,128)(2,1)} %get-tuple-element.11.weights), custom_call_target="tpu_custom_call" | custom-call | tf_op jit(solution)/shard_map/pallas_call | solution.py:596
  326.8 1.4 copy.33
  328.2 0.3 reshape.12
  328.5 0.8 slice.4
  (5 shorter events, 0.0 us)

commit v4 on v3

--- a/solution.py
+++ b/solution.py
@@ -283,7 +283,7 @@
             place[g, pl.ds(b * ROWS, ROWS), :] = hit.astype(F32).astype(BF16)
             return 0
 
-        lax.fori_loop(0, 64, block, 0)
+        lax.fori_loop(0, 64, block, 0, unroll=4)
 
         def clear(e, _):
             acc[e] = jnp.zeros((256, 256), F32)
@@ -301,7 +301,7 @@
             rows[:, pl.ds(g * 16, 16), :] = picked.astype(BF16).reshape(EXP, 16, PW)
             return 0
 
-        lax.fori_loop(0, 16, group, 0)
+        lax.fori_loop(0, 16, group, 0, unroll=2)
 
     for i in range(PER_STEP):
         e = step * PER_STEP + i

time: 331 us -> 320 us (0.967)
  Pallas kernels: 322 us -> 311 us
    pallas_call x1, Pallas kernels: 76.3 us -> 65.9 us  [upward(): pl.pallas_call(upward_kernel, grid=(PARTS, EXP // PER_STEP), out_shape=[j...]
where the time goes in v4:
time: 320 us; the launch traced here: 319 us
  Pallas kernels  311 us (97%)
  local copies, waits for them, and re-layouts  5.83 us (2%)
    pallas_call x1, Pallas kernels, downward(): pl.pallas_call(downward_kernel, out_shape=[jax.ShapeDtypeStruct((CHUNKS,...  138 us
    pallas_call x1, Pallas kernels, gather(): pl.pallas_call(gather_kernel, out_shape=[jax.ShapeDtypeStruct((PARTS, 4,...  107 us
    pallas_call x1, Pallas kernels, upward(): pl.pallas_call(upward_kernel, grid=(PARTS, EXP // PER_STEP), out_shape=[j...  65.9 us

profile of v4, /device:TPU:0, one launch (start us, length us, event | category | flops | bytes accessed | tf_op | source)
XLA Modules:
  0.0 318.8 jit_solution(9734394036556991759)
XLA Ops:
  0.0 0.7 convert_convert_fusion
  0.7 0.7 fusion.1
  1.4 0.1 copy.28
  1.5 0.1 copy.29
  1.6 0.1 copy.27
  1.7 0.1 copy.26
  1.8 0.8 copy.25
  2.6 0.1 eq.15
  2.7 0.2 convert_reduce_fusion
  2.9 0.1 convert_element_type.16
  3.1 1.1 concatenate.6
  4.2 0.8 copy.36
  5.0 107.2 %shard_map.91 = (bf16[3,4,4,4,64,1024]{5,4,3,2,1,0:T(8,128)(2,1)}, bf16[32,3,96,3072]{3,2,1,0:T(8,128)(2,1)}) custom-call(bf16[3,64,1024]{2,1,0:T(8,128)(2,1)} %bitcast.18, bf16[45,32,2880]{2,1,0:T(8,128)(2,1)} %bitcast.14, bf16[45,32,90]{2,1,0:T(8,128)(2,1)} %bitcast.20, bf16[45,32,2880]{2,1,0:T(8,128)(2,1)} %bitcast.15, bf16[45,32,90]{2,1,0:T(8,128)(2,1)} %bitcast.21, ...), custom_call_target="tpu_custom_call" | custom-call | tf_op jit(solution)/shard_map/pallas_call | solution.py:238
  112.2 65.9 %shard_map.92 = (bf16[32,256,128]{2,1,0:T(8,128)(2,1)}, bf16[16,256,512]{2,1,0:T(8,128)(2,1)}) custom-call(bf16[3,4,4,4,64,1024]{5,4,3,2,1,0:T(8,128)(2,1)} %get-tuple-element.10.every.meta, bf16[3,4,4,4,64,1024]{5,4,3,2,1,0:T(8,128)(2,1)} %get-tuple-element.10.every.meta, bf16[32,3,96,3072]{3,2,1,0:T(8,128)(2,1)} %get-tuple-element.11.weights), custom_call_target="tpu_custom_call" | custom-call | tf_op jit(solution)/shard_map/pallas_call | solution.py:332
  178.2 138.2 %shard_map.93 = (bf16[2,3,64,512]{3,2,1,0:T(8,128)(2,1)}, bf16[2,3,4,4,4,64,512]{6,5,4,3,2,1,0:T(8,128)(2,1)}) custom-call(bf16[32,256,128]{2,1,0:T(8,128)(2,1)} %get-tuple-element.12.hidden, bf16[16,256,512]{2,1,0:T(8,128)(2,1)} %get-tuple-element.13.place, bf16[32,3,96,3072]{3,2,1,0:T(8,128)(2,1)} %get-tuple-element.11.weights), custom_call_target="tpu_custom_call" | custom-call | tf_op jit(solution)/shard_map/pallas_call | solution.py:596
  316.4 1.4 copy.33
  317.8 0.3 reshape.12
  318.1 0.8 slice.4
  (5 shorter events, 0.0 us)

commit v5 on v4

--- a/solution.py
+++ b/solution.py
@@ -289,7 +289,7 @@
             acc[e] = jnp.zeros((256, 256), F32)
             return 0
 
-        lax.fori_loop(0, EXP, clear, 0)
+        lax.fori_loop(0, EXP, clear, 0, unroll=4)
 
     @pl.when(step == 0)
     def _():
@@ -301,7 +301,7 @@
             rows[:, pl.ds(g * 16, 16), :] = picked.astype(BF16).reshape(EXP, 16, PW)
             return 0
 
-        lax.fori_loop(0, 16, group, 0, unroll=2)
+        lax.fori_loop(0, 16, group, 0, unroll=4)
 
     for i in range(PER_STEP):
         e = step * PER_STEP + i
@@ -398,7 +398,7 @@
                 results[:, pl.ds(first, 16), :] = y.astype(BF16).reshape(16, 16, CW)
             return 0
 
-        lax.fori_loop(0, BATCHES, batch, 0)
+        lax.fori_loop(0, BATCHES, batch, 0, unroll=2)
 
     def combine(c, p):
         def store(g):
@@ -416,7 +416,7 @@
             store(g).start()
             return 0
 
-        lax.fori_loop(0, 16, group, 0, unroll=2)
+        lax.fori_loop(0, 16, group, 0, unroll=4)
 
         def stored(g, _):
             store(g).wait()

time: 320 us -> 318 us (level)
  no operation moved by 1% of the time
where the time goes in v5:
time: 318 us; the launch traced here: 317 us
  Pallas kernels  309 us (97%)
  local copies, waits for them, and re-layouts  5.83 us (2%)
    pallas_call x1, Pallas kernels, downward(): pl.pallas_call(downward_kernel, out_shape=[jax.ShapeDtypeStruct((CHUNKS,...  138 us
    pallas_call x1, Pallas kernels, gather(): pl.pallas_call(gather_kernel, out_shape=[jax.ShapeDtypeStruct((PARTS, 4,...  107 us
    pallas_call x1, Pallas kernels, upward(): pl.pallas_call(upward_kernel, grid=(PARTS, EXP // PER_STEP), out_shape=[j...  63.6 us

profile of v5, /device:TPU:0, one launch (start us, length us, event | category | flops | bytes accessed | tf_op | source)
XLA Modules:
  0.0 316.6 jit_solution(12975684876490574362)
XLA Ops:
  0.0 0.7 convert_convert_fusion
  0.7 0.7 fusion.1
  1.4 0.1 copy.28
  1.5 0.1 copy.29
  1.6 0.1 copy.27
  1.7 0.1 copy.26
  1.8 0.8 copy.25
  2.6 0.1 eq.15
  2.7 0.2 convert_reduce_fusion
  2.9 0.1 convert_element_type.16
  3.1 1.1 concatenate.6
  4.2 0.8 copy.36
  5.0 107.2 %shard_map.91 = (bf16[3,4,4,4,64,1024]{5,4,3,2,1,0:T(8,128)(2,1)}, bf16[32,3,96,3072]{3,2,1,0:T(8,128)(2,1)}) custom-call(bf16[3,64,1024]{2,1,0:T(8,128)(2,1)} %bitcast.18, bf16[45,32,2880]{2,1,0:T(8,128)(2,1)} %bitcast.14, bf16[45,32,90]{2,1,0:T(8,128)(2,1)} %bitcast.20, bf16[45,32,2880]{2,1,0:T(8,128)(2,1)} %bitcast.15, bf16[45,32,90]{2,1,0:T(8,128)(2,1)} %bitcast.21, ...), custom_call_target="tpu_custom_call" | custom-call | tf_op jit(solution)/shard_map/pallas_call | solution.py:238
  112.2 63.6 %shard_map.92 = (bf16[32,256,128]{2,1,0:T(8,128)(2,1)}, bf16[16,256,512]{2,1,0:T(8,128)(2,1)}) custom-call(bf16[3,4,4,4,64,1024]{5,4,3,2,1,0:T(8,128)(2,1)} %get-tuple-element.10.every.meta, bf16[3,4,4,4,64,1024]{5,4,3,2,1,0:T(8,128)(2,1)} %get-tuple-element.10.every.meta, bf16[32,3,96,3072]{3,2,1,0:T(8,128)(2,1)} %get-tuple-element.11.weights), custom_call_target="tpu_custom_call" | custom-call | tf_op jit(solution)/shard_map/pallas_call | solution.py:332
  175.9 138.2 %shard_map.93 = (bf16[2,3,64,512]{3,2,1,0:T(8,128)(2,1)}, bf16[2,3,4,4,4,64,512]{6,5,4,3,2,1,0:T(8,128)(2,1)}) custom-call(bf16[32,256,128]{2,1,0:T(8,128)(2,1)} %get-tuple-element.12.hidden, bf16[16,256,512]{2,1,0:T(8,128)(2,1)} %get-tuple-element.13.place, bf16[32,3,96,3072]{3,2,1,0:T(8,128)(2,1)} %get-tuple-element.11.weights), custom_call_target="tpu_custom_call" | custom-call | tf_op jit(solution)/shard_map/pallas_call | solution.py:596
  314.1 1.4 copy.33
  315.5 0.3 reshape.12
  315.8 0.8 slice.4
  (5 shorter events, 0.0 us)
